TPU v7x, 256 devices: a whole 4x4x8 slice. The times are simulated.
256 devices in a mesh: dp: 8 (over z), eslice: 32 (over x, y, core).
Axes of the slice: x: 4, y: 4, z: 8, core: 2. Of those that a mesh axis runs over, the one named last changes fastest.
Arguments:
- inputs: bfloat16 [32768, 2048], P(('dp', 'eslice')), may hold values from -6 to 6
- cotangent: bfloat16 [32768, 2048], P(('dp', 'eslice')), may hold values from -6 to 6
- routes: int32 [32768, 2], P(('dp', 'eslice')), may hold values from 0 to 15, all different within a row; in each aligned block of 128 rows (0 to 127, 128 to 255, ...) at most 20 rows name the same one
- gate_weights: bfloat16 [32768, 2], P(('dp', 'eslice')), may hold values from 0.049804688 to 1
- gate_weight: bfloat16 [64, 2048, 256], P('eslice', 'dp'), may hold values from -0.125 to 0.125
- up_weight: bfloat16 [64, 2048, 256], P('eslice', 'dp'), may hold values from -0.125 to 0.125
- down_weight: bfloat16 [64, 2048, 256], P('eslice', 'dp'), may hold values from -0.09375 to 0.09375
Outputs:
- input_grad: bfloat16 [32768, 2048], P(('dp', 'eslice'))
- gate_grad: float32 [32768, 2], P(('dp', 'eslice'))
- gate_weight_grad: bfloat16 [64, 2048, 256], P('eslice', 'dp')
- up_weight_grad: bfloat16 [64, 2048, 256], P('eslice', 'dp')
- down_weight_grad: bfloat16 [64, 2048, 256], P('eslice', 'dp')
Inputs may be any that keep to these rules, and one draw needn't show every extreme that they name: In the 256 routes of one device's tokens no expert is named more than 20 times, a bound that some block reaches; a token's 2 experts differ; every expert is named somewhere.
All inputs are finite; a program needn't handle non-finite values.
Results may differ from a plain program's by a relative error of at most 0.017.
Values may be sent and summed in bfloat16 or wider, within the bound.
No kernel may reach another device: no remote copies, remote signals or barrier semaphores. Data moves between devices by JAX's collectives and lax.ppermute only.
A program may use at most 128 MiB of HBM per device.

v0:
```python
import functools

import jax
import jax.numpy as jnp
from jax import lax
from jax.experimental import pallas as pl
from jax.experimental.pallas import tpu as pltpu
from jax.sharding import PartitionSpec as P

BF = jnp.bfloat16
F32 = jnp.float32
T = 128
D = 2048
E = 16
SRC = 32
MAIN = 16
REST = 4
ROWS = SRC * (MAIN + REST)
FULL = SRC * MAIN
CB = 256
MB = 1 << 20


def iota(shape, dim):
    return lax.broadcasted_iota(jnp.int32, shape, dim)


def dot(a, b, ca=1, cb=0):
    return lax.dot_general(a, b, (((ca,), (cb,)), ((), ())), preferred_element_type=F32)


def slots(routes):
    lane = iota((T, 128), 1)
    first = routes[:, 0:1] == lane
    second = routes[:, 1:2] == lane
    member = jnp.logical_or(first, second)
    before = (iota((T, T), 1) < iota((T, T), 0)).astype(BF)
    position = dot(before, member.astype(F32).astype(BF))
    return first, second, jnp.where(member, position, -1.0)


def send_kernel(routes_ref, gates_ref, x_ref, dy_ref, sx_ref, sdy_ref):
    first, second, slot = slots(routes_ref[...])
    gates = gates_ref[...].astype(F32)
    gate = jnp.where(first, gates[:, 0:1], 0.0) + jnp.where(second, gates[:, 1:2], 0.0)
    count = E * MAIN
    expand = (iota((count, 128), 0) // MAIN == iota((count, 128), 1)).astype(F32).astype(BF)
    slot_row = dot(expand, slot.T.astype(BF))
    gate_row = dot(expand, gate.T.astype(BF))
    row = iota((count, T), 0)
    main = slot_row == (row % MAIN).astype(F32)
    rest = slot_row == (row % REST + MAIN).astype(F32)
    block = row // REST % 4

    def emit(values, src_ref, out_ref):
        pick = jnp.where(main, values, 0.0).astype(BF)
        picks = [jnp.where(jnp.logical_and(rest, block == k), values, 0.0).astype(BF) for k in range(4)]
        for half in range(2):
            left = None
            for k in range(4):
                cols = src_ref[:, half * 1024 + k * CB:half * 1024 + (k + 1) * CB]
                got = dot(pick, cols).astype(BF)
                out_ref[:, half, k * MAIN:(k + 1) * MAIN, :] = got.reshape(E, MAIN, CB)
                more = dot(picks[k], cols)
                left = more if left is None else left + more
            out_ref[:, half, 4 * MAIN:5 * MAIN, :] = left.astype(BF).reshape(E, MAIN, CB)

    emit(jnp.ones((count, T), F32), x_ref, sx_ref)
    emit(gate_row, dy_ref, sdy_ref)


def rest_pick(k):
    shape = (SRC * REST, FULL)
    r, c = iota(shape, 0), iota(shape, 1)
    hit = jnp.logical_and(r // REST == c // MAIN, r % REST == c % REST)
    return jnp.logical_and(hit, c // REST % 4 == k).astype(F32).astype(BF)


def assemble_kernel(core_ref, mine_ref, other_ref, out_ref):
    core = core_ref[0]
    for ref, half in ((mine_ref, core), (other_ref, 1 - core)):
        left = ref[:, 4 * MAIN:5 * MAIN, :].reshape(FULL, CB)
        for k in range(4):
            cols = pl.ds(pl.multiple_of(half * 1024 + k * CB, CB), CB)
            out_ref[0:FULL, cols] = ref[:, k * MAIN:(k + 1) * MAIN, :].reshape(FULL, CB)
            out_ref[FULL:ROWS, cols] = dot(rest_pick(k), left).astype(BF)


def main_kernel(x_ref, dy_ref, w_ref, dgate_ref, dup_ref, gate_ref, grad_ref, hid_ref):
    q = pl.program_id(0)
    step = 128
    wg = w_ref[:, 0, 0].reshape(D, CB)
    wu = w_ref[:, 0, 1].reshape(D, CB)
    wd = w_ref[:, 0, 2].reshape(D, CB)
    for at in range(0, ROWS, step):
        rows = slice(at, at + step)
        gpre = dot(x_ref[rows, :], wg)
        upre = dot(x_ref[rows, :], wu)
        zeta = dot(dy_ref[rows, :], wd)
        sig = jax.nn.sigmoid(gpre)
        act = gpre * sig
        hidden = (act * upre).astype(BF)
        hid_ref[rows, :] = hidden
        part = jnp.sum(hidden.astype(F32) * zeta, axis=1, keepdims=True)
        part = jnp.broadcast_to(part, (step, 128))

        @pl.when(q == 0)
        def _():
            gate_ref[rows, :] = part

        @pl.when(q != 0)
        def _():
            gate_ref[rows, :] += part

        dgate_ref[0, rows, :] = (zeta * upre * sig * (1.0 + gpre * (1.0 - sig))).astype(BF)
        dup_ref[0, rows, :] = (zeta * act).astype(BF)
    for m, (left, right) in enumerate(
        ((dgate_ref[0], x_ref), (dup_ref[0], x_ref), (hid_ref[...], dy_ref))
    ):
        for d in range(8):
            grad_ref[d, 0, m] = dot(left, right[:, d * CB:(d + 1) * CB], 0, 0).astype(BF)


def back_kernel(dgate_ref, dup_ref, gate_ref, w_ref, out_ref):
    picks = [rest_pick(k) for k in range(4)]
    for group in range(2):
        left = None
        for k in range(4):
            d = group * 4 + k
            total = None
            for q in range(2):
                a = dot(dgate_ref[q], w_ref[d, q, 0], 1, 1)
                b = dot(dup_ref[q], w_ref[d, q, 1], 1, 1)
                total = a + b if total is None else total + a + b
            rows = total.astype(BF)
            out_ref[:, d * MAIN:(d + 1) * MAIN, :] = rows[0:FULL].reshape(SRC, MAIN, CB)
            more = dot(picks[k], rows[FULL:ROWS], 0, 0)
            left = more if left is None else left + more
        at = (8 + group) * MAIN
        out_ref[:, at:at + MAIN, :] = left.astype(BF).reshape(SRC, MAIN, CB)
    gates = gate_ref[...].astype(BF)
    out_ref[:, 10 * MAIN:11 * MAIN, 0:128] = gates[0:FULL].reshape(SRC, MAIN, 128)
    spread = dot(picks[0], gates[FULL:ROWS], 0, 0).astype(BF)
    out_ref[:, 10 * MAIN:11 * MAIN, 128:256] = spread.reshape(SRC, MAIN, 128)


def combine_kernel(routes_ref, gates_ref, back_ref, grad_ref, gate_ref):
    first, second, slot = slots(routes_ref[...])
    gates = gates_ref[...].astype(F32)
    count = 2 * E * MAIN
    expand = (iota((128, count), 1) // (2 * MAIN) == iota((128, count), 0)).astype(F32).astype(BF)
    col = iota((T, count), 1)
    main_at = (col % MAIN).astype(F32)
    rest_at = (col % REST + MAIN).astype(F32)
    block = col // REST % 4
    slot_col = dot(slot.astype(BF), expand)
    main = (slot_col == main_at).astype(F32).astype(BF)
    rest = slot_col == rest_at
    rests = [jnp.logical_and(rest, block == k).astype(F32).astype(BF) for k in range(4)]
    for d in range(8):
        got = back_ref[:, d * MAIN:(d + 1) * MAIN, :].reshape(count, CB)
        at = (8 + d // 4) * MAIN
        more = back_ref[:, at:at + MAIN, :].reshape(count, CB)
        grad_ref[:, d * CB:(d + 1) * CB] = (dot(main, got) + dot(rests[d % 4], more)).astype(BF)
    parts = back_ref[:, 10 * MAIN:11 * MAIN, :].reshape(count, CB)
    columns = []
    for k, chosen in enumerate((first, second)):
        own = dot(jnp.where(chosen, slot, -1.0).astype(BF), expand)
        own = jnp.where(dot(chosen.astype(F32).astype(BF), expand) > 0.5, own, -1.0)
        a = (own == main_at).astype(F32).astype(BF)
        b = jnp.logical_and(own == rest_at, block == 0).astype(F32).astype(BF)
        value = dot(a, parts[:, 0:128]) + dot(b, parts[:, 128:256])
        columns.append(value[:, 0:1] / gates[:, k:k + 1])
    gate_ref[...] = jnp.concatenate(columns, axis=1)


def vmem(count):
    return [pl.BlockSpec(memory_space=pltpu.VMEM)] * count


def params():
    return pltpu.CompilerParams(vmem_limit_bytes=48 * MB)


def cost(flops, moved):
    return pl.CostEstimate(flops=flops, bytes_accessed=moved, transcendentals=0)


def shape(*sizes, dtype=BF):
    return jax.ShapeDtypeStruct(sizes, dtype)


def per_device(inputs, cotangent, routes, gate_weights, gate_weight, up_weight, down_weight):
    here = lax.axis_index("eslice")
    core = here % 2
    side = here // 2 % 2

    stacked = jnp.stack((gate_weight, up_weight, down_weight), axis=1)
    own = lax.dynamic_index_in_dim(stacked, side, 0, keepdims=False)
    away = lax.dynamic_index_in_dim(stacked, 1 - side, 0, keepdims=False)
    swap = [(i, i ^ 2) for i in range(SRC)]
    partner = [(i, i ^ 1) for i in range(SRC)]
    came = lax.ppermute(away, "eslice", swap)
    weights = lax.all_gather(jnp.stack((own, came)), "dp", axis=0, tiled=False)

    send_x, send_dy = pl.pallas_call(
        send_kernel,
        out_shape=(shape(E, 2, 5 * MAIN, CB), shape(E, 2, 5 * MAIN, CB)),
        in_specs=vmem(4),
        out_specs=tuple(vmem(2)),
        compiler_params=params(),
        cost_estimate=cost(10**9, 4 * MB),
        name="send",
    )(routes, gate_weights, inputs, cotangent)

    def dispatch(values):
        mine = lax.all_to_all(values.reshape(SRC, 5 * MAIN, CB), "eslice", 0, 0, tiled=True)
        other = lax.ppermute(mine, "eslice", partner)
        return pl.pallas_call(
            assemble_kernel,
            out_shape=shape(ROWS, D),
            in_specs=[pl.BlockSpec(memory_space=pltpu.SMEM)] + vmem(2),
            out_specs=pl.BlockSpec(memory_space=pltpu.VMEM),
            compiler_params=params(),
            cost_estimate=cost(10**9, 5 * MB),
            name="assemble",
        )(core.reshape(1), mine, other)

    rows_x = dispatch(send_x)
    rows_dy = dispatch(send_dy)

    dgate, dup, gate_part, grads = pl.pallas_call(
        main_kernel,
        grid=(2,),
        out_shape=(
            shape(2, ROWS, CB),
            shape(2, ROWS, CB),
            shape(ROWS, 128, dtype=F32),
            shape(8, 2, 3, CB, CB),
        ),
        in_specs=[
            pl.BlockSpec((ROWS, D), lambda q: (0, 0)),
            pl.BlockSpec((ROWS, D), lambda q: (0, 0)),
            pl.BlockSpec((8, 1, 3, CB, CB), lambda q: (0, q, 0, 0, 0)),
        ],
        out_specs=(
            pl.BlockSpec((1, ROWS, CB), lambda q: (q, 0, 0)),
            pl.BlockSpec((1, ROWS, CB), lambda q: (q, 0, 0)),
            pl.BlockSpec((ROWS, 128), lambda q: (0, 0)),
            pl.BlockSpec((8, 1, 3, CB, CB), lambda q: (0, q, 0, 0, 0)),
        ),
        scratch_shapes=[pltpu.VMEM((ROWS, CB), BF)],
        compiler_params=params(),
        cost_estimate=cost(8 * 10**9, 20 * MB),
        name="main",
    )(rows_x, rows_dy, weights)

    back = pl.pallas_call(
        back_kernel,
        out_shape=shape(SRC, 11 * MAIN, CB),
        in_specs=vmem(4),
        out_specs=pl.BlockSpec(memory_space=pltpu.VMEM),
        compiler_params=params(),
        cost_estimate=cost(3 * 10**9, 10 * MB),
        name="back",
    )(dgate, dup, gate_part, weights)
    returned = lax.all_to_all(back, "eslice", 0, 0, tiled=True)
    input_grad, gate_grad = pl.pallas_call(
        combine_kernel,
        out_shape=(shape(T, D), shape(T, 2, dtype=F32)),
        in_specs=vmem(3),
        out_specs=tuple(vmem(2)),
        compiler_params=params(),
        cost_estimate=cost(10**9, 4 * MB),
        name="combine",
    )(routes, gate_weights, returned)

    reduced = lax.psum_scatter(grads, "dp", scatter_dimension=0, tiled=False)
    kept = reduced[0]
    came = lax.ppermute(reduced[1], "eslice", swap)
    low = jnp.where(side == 0, kept, came)
    high = jnp.where(side == 0, came, kept)
    out = jnp.stack((low, high), axis=1).swapaxes(2, 3)
    return (input_grad, gate_grad, out[0], out[1], out[2])


def solution(mesh):
    token = P(("dp", "eslice"), None)
    weight = P("eslice", "dp", None)
    return jax.shard_map(
        per_device,
        mesh=mesh,
        in_specs=(token,) * 4 + (weight,) * 3,
        out_specs=(token,) * 2 + (weight,) * 3,
        check_vma=False,
    )
```

profile of v0, /device:TPU:1, one launch (start us, length us, event | category | flops | bytes accessed | tf_op | source)
XLA Modules:
  0.0 220.8 jit_solution(6582243680606466359)
XLA Ops:
  7.2 0.0 all-gather.3.cloned.1.call-start
  7.3 1.3 pad_maximum_fusion
  8.6 0.1 constant_dynamic-slice_fusion
  8.6 2.2 %collective-permute-start.2 = (bf16[3,256,256]{2,1,0:T(8,128)(2,1)S(1)}, bf16[3,256,256]{2,1,0:T(8,128)(2,1)S(1)}, u32[]{:S(2)}, u32[]{:S(2)}) collective-permute-start(bf16[3,256,256]{2,1,0:T(8,128)(2,1)S(1)} %get-tuple-element.32), channel_id=1, source_target_pairs={{0,2},{1,3},{2,0},{3,1},{4,6},{5,7},{6,4},{7,5},{8,10},{9,11},{10,... | collective-permute-start | bytes 1179656 | tf_op jit(solution)/shard_map/ppermute | solution.py:203
  10.9 7.6 %collective-permute-done.2 = bf16[3,256,256]{2,1,0:T(8,128)(2,1)S(1)} collective-permute-done((bf16[3,256,256]{2,1,0:T(8,128)(2,1)S(1)}, bf16[3,256,256]{2,1,0:T(8,128)(2,1)S(1)}, u32[]{:S(2)}, u32[]{:S(2)}) %collective-permute-start.2) | collective-permute-done | bytes 393248 | tf_op jit(solution)/shard_map/ppermute | solution.py:203
  18.5 1.0 pad_maximum_fusion.1
  19.4 0.0 all-gather.3.cloned.1.call-update
  19.4 0.0 copy-done.12
  19.4 0.1 copy.16.gates_ref
  19.6 0.0 copy-done.11
  19.6 0.1 copy.15.routes_ref
  19.7 1.7 send.1
  21.4 29.8 %all_to_all.15.mine_ref = bf16[32,80,256]{2,1,0:T(8,128)(2,1)S(1)} all-to-all(bf16[32,80,256]{2,1,0:T(8,128)(2,1)S(1)} %bitcast.31), channel_id=1, replica_groups=mesh['dp'=8,'eslice'=32] {'eslice'}, dimensions={0} | all-to-all | bytes 2621440 | tf_op jit(solution)/shard_map/all_to_all | solution.py:217
  51.2 3.8 %all-to-all-start.1 = ((bf16[32,80,256]{2,1,0:T(8,128)(2,1)}), bf16[32,80,256]{2,1,0:T(8,128)(2,1)S(1)}, u32[]{:S(2)}, u32[]{:S(2)}) async-start(bf16[32,80,256]{2,1,0:T(8,128)(2,1)} %bitcast.30), calls=%async_computation.1 | async-start | bytes 2621440 | tf_op jit(solution)/shard_map/all_to_all | solution.py:217
  55.0 0.0 reduce-scatter.2.cloned.1.call-start
  55.0 0.4 collective-permute-start
  55.4 19.4 %all-to-all-done.1.mine_ref = bf16[32,80,256]{2,1,0:T(8,128)(2,1)S(1)} async-done(((bf16[32,80,256]{2,1,0:T(8,128)(2,1)}), bf16[32,80,256]{2,1,0:T(8,128)(2,1)S(1)}, u32[]{:S(2)}, u32[]{:S(2)}) %all-to-all-start.1) | async-done | bytes 1310752 | tf_op jit(solution)/shard_map/all_to_all | solution.py:217
  74.8 0.4 collective-permute-start.1
  75.2 0.0 collective-permute-done.other_ref
  75.2 2.0 assemble.2.x_ref
  77.2 1.5 copy-done.1
  78.7 0.0 collective-permute-done.1.other_ref
  78.7 2.0 assemble.3.dy_ref
  80.7 1.5 copy-done.3
  82.2 16.8 %all-gather.3.cloned.1.call-done = bf16[16,3,256,256]{3,2,0,1:T(8,128)(2,1)} async-done(((bf16[2,3,256,256]{3,2,0,1:T(8,128)(2,1)}), bf16[16,3,256,256]{3,2,0,1:T(8,128)(2,1)}) %all-gather.3.cloned.1.call-update) | async-done | bytes 6291472 | tf_op jit(solution)/shard_map/all_gather | solution.py:204
  99.0 6.1 %copy.14 = bf16[16,3,256,256]{3,2,1,0:T(8,128)(2,1)} copy(bf16[16,3,256,256]{3,2,0,1:T(8,128)(2,1)} %all-gather.3.cloned.1.call-done) | data formatting | bytes 12582912 | tf_op jit(solution)/shard_map/all_gather | solution.py:204
  105.1 18.0 %main.1 = (bf16[2,640,256]{2,1,0:T(8,128)(2,1)S(1)}, bf16[2,640,256]{2,1,0:T(8,128)(2,1)S(1)}, f32[640,128]{1,0:T(8,128)S(1)}, bf16[8,2,3,256,256]{4,3,2,1,0:T(8,128)(2,1)}) custom-call(bf16[640,2048]{1,0:T(8,128)(2,1)S(1)} %copy-done.2, bf16[640,2048]{1,0:T(8,128)(2,1)} %copy-done.3, bf16[8,2,3,256,256]{4,3,2,1,0:T(8,128)(2,1)} %bitcast.32), custom_call_target="tpu_custom_call" | custom-call | flops 8000000000 | bytes 20971520 | tf_op jit(solution)/shard_map/main/pallas_call | solution.py:232
  123.2 0.8 copy-done.7
  124.0 0.9 copy-done.9
  124.9 0.0 reduce-scatter.2.cloned.1.call-update
  124.9 1.1 copy-done.8
  126.0 0.2 copy-done.10
  126.2 7.6 %back.1 = bf16[32,176,256]{2,1,0:T(8,128)(2,1)S(1)} custom-call(bf16[2,640,256]{2,1,0:T(8,128)(2,1)S(1)} %copy-done.8, bf16[2,640,256]{2,1,0:T(8,128)(2,1)S(1)} %copy-done.10, f32[640,128]{1,0:T(8,128)S(1)} %get-tuple-element.17.gate_ref, bf16[8,2,3,256,256]{4,3,2,1,0:T(8,128)(2,1)} %bitcast.33), custom_call_target="tpu_custom_call" | custom-call | flops 3000000000 | bytes 10485760 | tf_op jit(solution)/shard_map/back/pallas_call | solution.py:258
  133.8 1.6 copy-done
  135.5 7.5 %all-to-all-start.2 = ((bf16[32,176,256]{2,1,0:T(8,128)(2,1)}), bf16[32,176,256]{2,1,0:T(8,128)(2,1)S(1)}, u32[]{:S(2)}, u32[]{:S(2)}) async-start(bf16[32,176,256]{2,1,0:T(8,128)(2,1)} %copy-done), calls=%async_computation.2 | async-start | bytes 5767168 | tf_op jit(solution)/shard_map/all_to_all | solution.py:267
  143.0 55.9 %reduce-scatter.2.cloned.1.call-done = bf16[1,2,3,256,256]{4,3,2,1,0:T(8,128)(2,1)} async-done(((bf16[8,2,3,256,256]{4,3,2,1,0:T(8,128)(2,1)}), bf16[1,2,3,256,256]{4,3,2,1,0:T(8,128)(2,1)}) %reduce-scatter.2.cloned.1.call-update) | async-done | bytes 786448 | tf_op jit(solution)/shard_map/reduce_scatter | solution.py:278
  198.8 1.0 slice_bitcast_fusion
  199.9 1.3 collective-permute-start.3
  201.2 0.0 all-to-all-done.2.back_ref
  201.2 2.2 %combine.1 = (bf16[128,2048]{1,0:T(8,128)(2,1)}, f32[128,2]{1,0:T(8,128)S(1)}) custom-call(s32[128,2]{1,0:T(8,128)S(1)} %copy.15.routes_ref, bf16[128,2]{1,0:T(8,128)(2,1)S(1)} %copy.16.gates_ref, bf16[32,176,256]{2,1,0:T(8,128)(2,1)S(1)} %all-to-all-done.2.back_ref), custom_call_target="tpu_custom_call" | custom-call | flops 1000000000 | bytes 4194304 | tf_op jit(solution)/shard_map/combine/pallas_call | solution.py:268
  203.4 0.6 copy.17
  204.0 6.1 %collective-permute-done.3 = bf16[3,256,256]{2,1,0:T(8,128)(2,1)} collective-permute-done((bf16[3,256,256]{2,1,0:T(8,128)(2,1)S(1)}, bf16[3,256,256]{2,1,0:T(8,128)(2,1)}, u32[]{:S(2)}, u32[]{:S(2)}) %collective-permute-start.3) | collective-permute-done | bytes 393248 | tf_op jit(solution)/shard_map/ppermute | solution.py:280
  210.1 1.2 select_bitcast_fusion.1
  211.3 0.1 maximum_bitcast_fusion
  211.4 0.1 slice_bitcast_fusion.2
  211.4 0.8 copy.20
  212.3 0.8 copy.19
  213.1 0.8 copy.18
  (17 shorter events, 0.0 us)
Async XLA Ops:
  7.2 91.8 %all-gather.3.cloned.1.call-start = ((), (), s32[]{:S(2)}) async-start(), calls=%async_computation.5 | async-start | bytes 7077888 | tf_op jit(solution)/shard_map/all_gather | solution.py:204
  7.3 12.2 %copy-start.12 = (bf16[128,2]{0,1:T(2,128)(2,1)S(1)}, bf16[128,2]{0,1:T(2,128)(2,1)}, u32[]{:S(2)}) copy-start(bf16[128,2]{0,1:T(2,128)(2,1)} %param.10) | copy-start | bytes 1540
  7.3 12.3 %copy-start.11 = (s32[128,2]{0,1:T(2,128)S(1)}, s32[128,2]{0,1:T(2,128)}, u32[]{:S(2)}) copy-start(s32[128,2]{0,1:T(2,128)} %param.9) | copy-start | bytes 3076
  7.3 12.4 %copy-start.5 = (bf16[128,2048]{1,0:T(8,128)(2,1)S(1)}, bf16[128,2048]{1,0:T(8,128)(2,1)}, u32[]{:S(2)}) copy-start(bf16[128,2048]{1,0:T(8,128)(2,1)} %x_ref.1) | copy-start | bytes 1572868
  7.3 12.4 %copy-start.6 = (bf16[128,2048]{1,0:T(8,128)(2,1)S(1)}, bf16[128,2048]{1,0:T(8,128)(2,1)}, u32[]{:S(2)}) copy-start(bf16[128,2048]{1,0:T(8,128)(2,1)} %dy_ref.1) | copy-start | bytes 1572868
  8.6 9.8 %collective-permute-start.2 = (bf16[3,256,256]{2,1,0:T(8,128)(2,1)S(1)}, bf16[3,256,256]{2,1,0:T(8,128)(2,1)S(1)}, u32[]{:S(2)}, u32[]{:S(2)}) collective-permute-start(bf16[3,256,256]{2,1,0:T(8,128)(2,1)S(1)} %get-tuple-element.32), channel_id=1, source_target_pairs={{0,2},{1,3},{2,0},{3,1},{4,6},{5,7},{6,4},{7,5},{8,10},{9,11},{10,... | collective-permute-start | bytes 1179656 | tf_op jit(solution)/shard_map/ppermute | solution.py:203
  21.4 29.8 %copy-start.4 = (bf16[16,2,80,256]{3,2,1,0:T(8,128)(2,1)}, bf16[16,2,80,256]{3,2,1,0:T(8,128)(2,1)S(1)}, u32[]{:S(2)}) copy-start(bf16[16,2,80,256]{3,2,1,0:T(8,128)(2,1)S(1)} %get-tuple-element.14) | copy-start | bytes 3932164
  51.2 23.7 %all-to-all-start.1 = ((bf16[32,80,256]{2,1,0:T(8,128)(2,1)}), bf16[32,80,256]{2,1,0:T(8,128)(2,1)S(1)}, u32[]{:S(2)}, u32[]{:S(2)}) async-start(bf16[32,80,256]{2,1,0:T(8,128)(2,1)} %bitcast.30), calls=%async_computation.1 | async-start | bytes 2621440 | tf_op jit(solution)/shard_map/all_to_all | solution.py:217
  55.0 143.9 %reduce-scatter.2.cloned.1.call-start = ((), (), s32[]{:S(2)}) async-start(), calls=%async_computation.4 | async-start | bytes 7077888 | tf_op jit(solution)/shard_map/reduce_scatter | solution.py:278
  55.0 20.2 %collective-permute-start = (bf16[32,80,256]{2,1,0:T(8,128)(2,1)S(1)}, bf16[32,80,256]{2,1,0:T(8,128)(2,1)}, u32[]{:S(2)}, u32[]{:S(2)}) collective-permute-start(bf16[32,80,256]{2,1,0:T(8,128)(2,1)S(1)} %all_to_all.15.mine_ref), channel_id=1, source_target_pairs={{0,1},{1,0},{2,3},{3,2},{4,5},{5,4},{6,7},{7,6},{8,9},{9,8},{10,11... | collective-permute-start | bytes 3932168 | tf_op jit(solution)/shard_map/ppermute | solution.py:218
  74.8 3.9 %collective-permute-start.1 = (bf16[32,80,256]{2,1,0:T(8,128)(2,1)S(1)}, bf16[32,80,256]{2,1,0:T(8,128)(2,1)}, u32[]{:S(2)}, u32[]{:S(2)}) collective-permute-start(bf16[32,80,256]{2,1,0:T(8,128)(2,1)S(1)} %all-to-all-done.1.mine_ref), channel_id=1, source_target_pairs={{0,1},{1,0},{2,3},{3,2},{4,5},{5,4},{6,7},{7,6},{8,9},{9,8},{10,11... | collective-permute-start | bytes 3932168 | tf_op jit(solution)/shard_map/ppermute | solution.py:218
  77.2 1.5 copy-start.1
  80.7 1.5 copy-start.3
  82.2 22.9 %copy-start.2 = (bf16[640,2048]{1,0:T(8,128)(2,1)S(1)}, bf16[640,2048]{1,0:T(8,128)(2,1)}, u32[]{:S(2)}) copy-start(bf16[640,2048]{1,0:T(8,128)(2,1)} %copy-done.1) | copy-start | bytes 7864324
  123.2 0.8 copy-start.7
  124.0 0.9 copy-start.9
  124.9 1.1 copy-start.8
  124.9 1.3 copy-start.10
  133.8 1.6 copy-start
  135.5 65.7 %all-to-all-start.2 = ((bf16[32,176,256]{2,1,0:T(8,128)(2,1)}), bf16[32,176,256]{2,1,0:T(8,128)(2,1)S(1)}, u32[]{:S(2)}, u32[]{:S(2)}) async-start(bf16[32,176,256]{2,1,0:T(8,128)(2,1)} %copy-done), calls=%async_computation.2 | async-start | bytes 5767168 | tf_op jit(solution)/shard_map/all_to_all | solution.py:267
  199.9 10.2 %collective-permute-start.3 = (bf16[3,256,256]{2,1,0:T(8,128)(2,1)S(1)}, bf16[3,256,256]{2,1,0:T(8,128)(2,1)}, u32[]{:S(2)}, u32[]{:S(2)}) collective-permute-start(bf16[3,256,256]{2,1,0:T(8,128)(2,1)S(1)} %slice_bitcast_fusion), channel_id=1, source_target_pairs={{0,2},{1,3},{2,0},{3,1},{4,6},{5,7},{6,4},{7,5},{8,10},{9,11},{10,... | collective-permute-start | bytes 1179656 | tf_op jit(solution)/shard_map/ppermute | solution.py:280
Sparse Core Ops, SparseCore 0:
  19.6 79.4 all-gather.2
  125.0 73.7 reduce-scatter.1
where the time goes:
time: 221 us
  waiting for transfers between devices  106 us (48%)
  Pallas kernels  33.5 us (15%)
  blocking collectives  29.8 us (13%)
  local copies, waits for them, and re-layouts  18.2 us (8%)
  starting transfers between devices  15.7 us (7%)
  between operations  14.3 us (6%)
  other arithmetic  3.49 us (2%)
    reduce_scatter x1, waiting for transfers between devices, per_device(): reduced = lax.psum_scatter(grads, 'dp', scatter_dimension=0, tiled=False)  55.9 us
    all_to_all x1, blocking collectives, dispatch(): lax.all_to_all(values.reshape(SRC, 5 * MAIN, CB), 'eslice', 0, 0, tiled=T...  29.8 us
    all_to_all x1, waiting for transfers between devices, dispatch(): lax.all_to_all(values.reshape(SRC, 5 * MAIN, CB), 'eslice', 0, 0, tiled=T...  19.4 us
    pallas_call x1, Pallas kernels, per_device(): pl.pallas_call(main_kernel, grid=(2,), out_shape=(shape(2, ROWS, CB), sha...  18 us
    all_gather x1, waiting for transfers between devices, per_device(): weights = lax.all_gather(jnp.stack((own, came)), 'dp', axis=0, tiled=False)  16.8 us
    unnamed x32, local copies, waits for them, and re-layouts  11 us
    pallas_call x1, Pallas kernels, per_device(): pl.pallas_call(back_kernel, out_shape=shape(SRC, 11 * MAIN, CB), in_specs...  7.64 us
    ppermute x1, waiting for transfers between devices, per_device(): came = lax.ppermute(away, 'eslice', swap)  7.59 us
  transfers between devices with their start and end apart: 8, of which 5 were waited for; matrix products, arithmetic and copies ran while one was open for 1% of the time, Pallas kernels for 6%

commit v1 on v0

v1 whole, which is shorter than its diff:
```python
import functools

import jax
import jax.numpy as jnp
from jax import lax
from jax.experimental import pallas as pl
from jax.experimental.pallas import tpu as pltpu
from jax.sharding import PartitionSpec as P

BF = jnp.bfloat16
F32 = jnp.float32
T = 128
D = 2048
E = 16
SRC = 32
MAIN = 16
REST = 4
ROWS = SRC * (MAIN + REST)
FULL = SRC * MAIN
CB = 256
MB = 1 << 20


def iota(shape, dim):
    return lax.broadcasted_iota(jnp.int32, shape, dim)


def dot(a, b, ca=1, cb=0):
    return lax.dot_general(a, b, (((ca,), (cb,)), ((), ())), preferred_element_type=F32)


def slots(routes):
    expert = iota((128, T), 0)
    first = routes[0:1, :] == expert
    second = routes[1:2, :] == expert
    member = jnp.logical_or(first, second)
    before = (iota((T, T), 0) < iota((T, T), 1)).astype(F32).astype(BF)
    position = dot(member.astype(F32).astype(BF), before)
    return first, second, jnp.where(member, position, -1.0)


def send_kernel(routes_ref, gates_ref, x_ref, dy_ref, out_ref):
    first, second, slot = slots(routes_ref[...])
    gates = gates_ref[...].astype(F32)
    gate = jnp.where(first, gates[0:1, :], 0.0) + jnp.where(second, gates[1:2, :], 0.0)
    count = E * MAIN
    expand = (iota((count, 128), 0) // MAIN == iota((count, 128), 1)).astype(F32).astype(BF)
    slot_row = dot(expand, slot.astype(BF))
    gate_row = dot(expand, gate.astype(BF))
    row = iota((count, T), 0)
    main = slot_row == (row % MAIN).astype(F32)
    rest = slot_row == (row % REST + MAIN).astype(F32)
    block = row // REST % 4

    def put(at, rows):
        rows = rows.astype(BF).reshape(E // 2, 2, MAIN, CB)
        for side in range(2):
            out_ref[:, side, :, at * MAIN:(at + 1) * MAIN, :] = rows

    for base, values, src_ref in ((0, 1.0, x_ref), (10, gate_row, dy_ref)):
        pick = jnp.where(main, values, 0.0).astype(BF)
        picks = [jnp.where(jnp.logical_and(rest, block == k), values, 0.0).astype(BF) for k in range(4)]
        for group in range(2):
            left = None
            for k in range(4):
                d = group * 4 + k
                cols = src_ref[:, d * CB:(d + 1) * CB]
                put(base + d, dot(pick, cols))
                more = dot(picks[k], cols)
                left = more if left is None else left + more
            put(base + 8 + group, left)


def rest_pick(k):
    shape = (SRC * REST, FULL)
    r, c = iota(shape, 0), iota(shape, 1)
    hit = jnp.logical_and(r // REST == c // MAIN, r % REST == c % REST)
    return jnp.logical_and(hit, c // REST % 4 == k).astype(F32).astype(BF)


def pack_kernel(core_ref, *refs):
    for i, ref in enumerate(refs[:6]):
        refs[6][i // 3, i % 3] = ref[core_ref[0]]


def unpack(rows_in, base, into, left_ref, sem):
    copies = []
    for d in range(8):
        copies.append(pltpu.make_async_copy(
            rows_in.at[:, pl.ds((base + d) * MAIN, MAIN)],
            into.at[pl.ds(0, SRC), :, pl.ds(d * CB, CB)], sem.at[d]))
    for group in range(2):
        copies.append(pltpu.make_async_copy(
            rows_in.at[:, pl.ds((base + 8 + group) * MAIN, MAIN)], left_ref.at[group], sem.at[8 + group]))
    return copies


def spread_rest(into, left_ref, picks):
    for d in range(8):
        left = left_ref[d // 4].reshape(FULL, CB)
        got = dot(picks[d % 4], left).astype(BF)
        into[SRC:ROWS // MAIN, :, d * CB:(d + 1) * CB] = got.reshape(ROWS // MAIN - SRC, MAIN, CB)


def main_kernel(rows_in, w_in, dgate_out, dup_out, gate_out, grad_out,
                x_ref, dy_ref, left_ref, w_ref, grad_ref, side_ref, pre_ref, gate_ref,
                x_sem, dy_sem, w_sem, out_sem, side_sem, gate_sem):
    x_copies = unpack(rows_in, 0, x_ref, left_ref.at[0], x_sem)
    dy_copies = unpack(rows_in, 10, dy_ref, left_ref.at[1], dy_sem)
    w_copies = [[[pltpu.make_async_copy(w_in.at[d, q, m], w_ref.at[q, m, d], w_sem.at[q, m, d])
                  for d in range(8)] for m in range(3)] for q in range(2)]
    batches = (
        x_copies + w_copies[0][0] + w_copies[0][1],
        w_copies[1][0] + w_copies[1][1],
        dy_copies + w_copies[0][2] + w_copies[1][2],
    )
    for batch in batches:
        for copy in batch:
            copy.start()
    picks = [rest_pick(k) for k in range(4)]
    outs = []
    for q in range(2):
        for copy in batches[q]:
            copy.wait()
        if q == 0:
            spread_rest(x_ref, left_ref.at[0], picks)
        x = x_ref[...].reshape(ROWS, D)
        pre_ref[q, 0] = dot(x, w_ref[q, 0].reshape(D, CB))
        pre_ref[q, 1] = dot(x, w_ref[q, 1].reshape(D, CB))
    for copy in batches[2]:
        copy.wait()
    spread_rest(dy_ref, left_ref.at[1], picks)
    for q in range(2):
        zeta = dot(dy_ref[...].reshape(ROWS, D), w_ref[q, 2].reshape(D, CB))
        gpre, upre = pre_ref[q, 0], pre_ref[q, 1]
        sig = jax.nn.sigmoid(gpre)
        act = gpre * sig
        hidden = (act * upre).astype(BF)
        side_ref[q, 2] = hidden
        part = jnp.sum(hidden.astype(F32) * zeta, axis=1, keepdims=True)
        part = jnp.broadcast_to(part, (ROWS, 128))
        gate_ref[...] = part if q == 0 else gate_ref[...] + part
        side_ref[q, 0] = (zeta * upre * sig * (1.0 + gpre * (1.0 - sig))).astype(BF)
        side_ref[q, 1] = (zeta * act).astype(BF)
        for d in range(8):
            for m, rows_ref in enumerate((x_ref, x_ref, dy_ref)):
                cols = rows_ref[:, :, d * CB:(d + 1) * CB].reshape(ROWS, CB)
                grad_ref[d, q, m] = dot(cols, side_ref[q, m], 0, 0).astype(BF)
            if d % 4 == 3:
                for done in range(d - 3, d + 1):
                    outs.append(pltpu.make_async_copy(
                        grad_ref.at[done, q], grad_out.at[done, q], out_sem.at[done, q]))
                    outs[-1].start()
            if d == 3:
                for m, out in enumerate((dgate_out, dup_out)):
                    outs.append(pltpu.make_async_copy(side_ref.at[q, m], out.at[q], side_sem.at[q, m]))
                    outs[-1].start()
    outs.append(pltpu.make_async_copy(gate_ref, gate_out, gate_sem.at[0]))
    outs[-1].start()
    for copy in outs:
        copy.wait()


def back_kernel(dgate_ref, dup_ref, gate_ref, w_in, out_ref, left_ref, w_ref, w_sem):
    copies = [pltpu.make_async_copy(w_in.at[:, q, m], w_ref.at[q, m], w_sem.at[q, m])
              for q in range(2) for m in range(2)]
    for copy in copies:
        copy.start()
    for copy in copies:
        copy.wait()
    picks = [rest_pick(k) for k in range(4)]
    for group in range(2):
        left = None
        for k in range(4):
            d = group * 4 + k
            total = dot(dgate_ref[0], w_ref[0, 0, d], 1, 1) + dot(dup_ref[0], w_ref[0, 1, d], 1, 1)
            total += dot(dgate_ref[1], w_ref[1, 0, d], 1, 1) + dot(dup_ref[1], w_ref[1, 1, d], 1, 1)
            rows = total.astype(BF)
            out_ref[:, d * MAIN:(d + 1) * MAIN, :] = rows[0:FULL].reshape(SRC, MAIN, CB)
            more = dot(picks[k], rows[FULL:ROWS], 0, 0)
            left = more if left is None else left + more
        at = (8 + group) * MAIN
        out_ref[:, at:at + MAIN, :] = left.astype(BF).reshape(SRC, MAIN, CB)
    gates = gate_ref[...].astype(BF)
    out_ref[:, 10 * MAIN:11 * MAIN, 0:128] = gates[0:FULL].reshape(SRC, MAIN, 128)
    spread = dot(picks[0], gates[FULL:ROWS], 0, 0).astype(BF)
    out_ref[:, 10 * MAIN:11 * MAIN, 128:256] = spread.reshape(SRC, MAIN, 128)


def finish_kernel(core_ref, kept_ref, came_ref, *out_refs):
    core = core_ref[0]
    for m, out_ref in enumerate(out_refs):
        out_ref[core] = kept_ref[0, m]
        out_ref[1 - core] = came_ref[1, m]


def combine_kernel(routes_ref, gates_ref, back_ref, grad_ref, gate_ref):
    first, second, slot = slots(routes_ref[...])
    gates = gates_ref[...].astype(F32)
    count = 2 * E * MAIN
    place = iota((128, count), 1)
    expand = (place // (4 * MAIN) * 2 + place // MAIN % 2 == iota((128, count), 0)).astype(F32).astype(BF)
    col = iota((T, count), 1)
    main_at = (col % MAIN).astype(F32)
    rest_at = (col % REST + MAIN).astype(F32)
    block = col // REST % 4
    slot_col = dot(slot.astype(BF), expand, 0, 0)
    main = (slot_col == main_at).astype(F32).astype(BF)
    rest = slot_col == rest_at
    rests = [jnp.logical_and(rest, block == k).astype(F32).astype(BF) for k in range(4)]
    for d in range(8):
        got = back_ref[:, d * MAIN:(d + 1) * MAIN, :].reshape(count, CB)
        at = (8 + d // 4) * MAIN
        more = back_ref[:, at:at + MAIN, :].reshape(count, CB)
        grad_ref[:, d * CB:(d + 1) * CB] = (dot(main, got) + dot(rests[d % 4], more)).astype(BF)
    parts = back_ref[:, 10 * MAIN:11 * MAIN, :].reshape(count, CB)
    for k, chosen in enumerate((first, second)):
        own = dot(jnp.where(chosen, slot, -1.0).astype(BF), expand, 0, 0)
        own = jnp.where(dot(chosen.astype(F32).astype(BF), expand, 0, 0) > 0.5, own, -1.0)
        a = (own == main_at).astype(F32).astype(BF)
        b = jnp.logical_and(own == rest_at, block == 0).astype(F32).astype(BF)
        value = dot(parts[:, 0:128], a, 0, 1) + dot(parts[:, 128:256], b, 0, 1)
        gate_ref[k:k + 1, :] = value[0:1, :] / gates[k:k + 1, :]


def vmem(count):
    return [pl.BlockSpec(memory_space=pltpu.VMEM)] * count


def params():
    return pltpu.CompilerParams(vmem_limit_bytes=60 * MB)


def cost(flops, moved):
    return pl.CostEstimate(flops=flops, bytes_accessed=moved, transcendentals=0)


def shape(*sizes, dtype=BF):
    return jax.ShapeDtypeStruct(sizes, dtype)


def call(kernel, name, outs, args, flops, moved, kinds=None, out_kinds=None, scratch=()):
    spaces = {"s": pltpu.SMEM, "v": pltpu.VMEM, "a": pl.ANY}
    kinds = kinds or "v" * len(args)
    out_kinds = out_kinds or "v" * len(outs)
    return pl.pallas_call(
        kernel,
        out_shape=tuple(outs),
        in_specs=[pl.BlockSpec(memory_space=spaces[k]) for k in kinds],
        out_specs=tuple(pl.BlockSpec(memory_space=spaces[k]) for k in out_kinds),
        scratch_shapes=list(scratch),
        compiler_params=params(),
        cost_estimate=cost(flops, moved),
        name=name,
    )(*args)


PARTNER = [(i, i ^ 1) for i in range(SRC)]


def per_device(inputs, cotangent, routes, gate_weights, gate_weight, up_weight, down_weight):
    core = (lax.axis_index("eslice") % 2).reshape(1)
    dma = pltpu.SemaphoreType.DMA
    mats = (gate_weight, up_weight, down_weight)

    theirs = [lax.ppermute(w, "eslice", PARTNER) for w in mats]
    (packed,) = call(pack_kernel, "pack", [shape(2, 3, CB, CB)], (core, *mats, *theirs), 0, 2 * MB,
                     kinds="svvvvvv")
    weights = lax.all_gather(packed, "dp", axis=0, tiled=False)

    (sent,) = call(send_kernel, "send", [shape(E // 2, 2, 2, 20 * MAIN, CB)],
                   (routes.T, gate_weights.T, inputs, cotangent), 10**9, 6 * MB)
    rows = lax.all_to_all(sent.reshape(SRC, 20 * MAIN, CB), "eslice", 0, 0, tiled=True)

    tiles = pltpu.VMEM((ROWS // MAIN, MAIN, D), BF)
    dgate, dup, gate_part, grads = call(
        main_kernel, "main",
        [shape(2, ROWS, CB), shape(2, ROWS, CB), shape(ROWS, 128, dtype=F32), shape(8, 2, 3, CB, CB)],
        (rows, weights), 8 * 10**9, 24 * MB, kinds="aa", out_kinds="aaaa",
        scratch=(tiles, tiles, pltpu.VMEM((2, 2, SRC, MAIN, CB), BF), pltpu.VMEM((2, 3, 8, CB, CB), BF),
                 pltpu.VMEM((8, 2, 3, CB, CB), BF), pltpu.VMEM((2, 3, ROWS, CB), BF),
                 pltpu.VMEM((2, 2, ROWS, CB), F32), pltpu.VMEM((ROWS, 128), F32),
                 dma((10,)), dma((10,)), dma((2, 3, 8)), dma((8, 2)), dma((2, 2)), dma((1,))))
    reduced = lax.psum_scatter(grads, "dp", scatter_dimension=0, tiled=False)

    (back,) = call(
        back_kernel, "back", [shape(SRC, 11 * MAIN, CB)], (dgate, dup, gate_part, weights),
        3 * 10**9, 12 * MB, kinds="vvva",
        scratch=(pltpu.VMEM((2, FULL, CB), F32), pltpu.VMEM((2, 2, 8, CB, CB), BF), dma((2, 2))))
    returned = lax.all_to_all(back, "eslice", 0, 0, tiled=True)
    input_grad, gate_grad = call(combine_kernel, "combine", [shape(T, D), shape(2, T, dtype=F32)],
                                 (routes.T, gate_weights.T, returned), 10**9, 4 * MB)

    reduced, input_grad = lax.optimization_barrier((reduced, input_grad))
    came = lax.ppermute(reduced, "eslice", PARTNER)
    grads = call(finish_kernel, "finish", [shape(2, CB, CB)] * 3,
                 (core, reduced, came), 10**6, 3 * MB, kinds="svv")
    return (input_grad, gate_grad.T, *grads)


def solution(mesh):
    token = P(("dp", "eslice"), None)
    weight = P("eslice", "dp", None)
    return jax.shard_map(
        per_device,
        mesh=mesh,
        in_specs=(token,) * 4 + (weight,) * 3,
        out_specs=(token,) * 2 + (weight,) * 3,
        check_vma=False,
    )
```

time: 221 us -> 197 us (0.89)
  waiting for transfers between devices: 106 us -> 22 us
  blocking collectives: 29.8 us -> 112 us
  local copies, waits for them, and re-layouts: 18.2 us -> 1.61 us
  starting transfers between devices: 15.7 us -> 4.53 us
  Pallas kernels: 33.5 us -> 42 us
  other arithmetic: 3.49 us -> 0 us
    all_to_all x1 -> x2, blocking collectives: 29.8 us -> 112 us  [the longest x1 67.7 us: per_device(): lax.all_to_all(sent.reshape(SRC, 20 * MAIN, CB), 'eslice', 0, 0, tiled=True)]
    reduce_scatter x1, waiting for transfers between devices: 55.9 us -> 15.5 us  [per_device(): reduced = lax.psum_scatter(grads, 'dp', scatter_dimension=0, tiled=False)]
    all_to_all x2 -> x0, waiting for transfers between devices: 19.4 us -> none  [the longest x1 19.4 us: dispatch(): lax.all_to_all(values.reshape(SRC, 5 * MAIN, CB), 'eslice', 0, 0, tiled=T...]
    all_gather x1, waiting for transfers between devices: 16.8 us -> 2.72 us  [per_device(): weights = lax.all_gather(packed, 'dp', axis=0, tiled=False)]
    all_to_all x2 -> x0, starting transfers between devices: 11.3 us -> none  [the longest x1 7.53 us: per_device(): returned = lax.all_to_all(back, 'eslice', 0, 0, tiled=True)]
    ppermute x4, waiting for transfers between devices: 13.7 us -> 3.73 us  [the longest x1 2.12 us: per_device(): came = lax.ppermute(reduced, 'eslice', PARTNER)]
    unnamed x32 -> x8, local copies, waits for them, and re-layouts: 11 us -> 1.61 us
    pallas_call x6, Pallas kernels: 33.5 us -> 42 us  [call(): pl.pallas_call(kernel, out_shape=tuple(outs), in_specs=[pl.BlockSpec(memo...]
  transfers between devices with their start and end apart: 8 -> 6, of which waited for: 5 -> 6; matrix products, arithmetic and copies ran while one was open for 1% -> 0% of each run, Pallas kernels for 6% -> 7%
where the time goes in v1:
time: 197 us; the launch traced here: 196 us
  blocking collectives  112 us (57%)
  Pallas kernels  42 us (21%)
  waiting for transfers between devices  22 us (11%)
  between operations  14.1 us (7%)
  starting transfers between devices  4.53 us (2%)
    all_to_all x1, blocking collectives, per_device(): lax.all_to_all(sent.reshape(SRC, 20 * MAIN, CB), 'eslice', 0, 0, tiled=True)  67.7 us
    all_to_all x1, blocking collectives, per_device(): returned = lax.all_to_all(back, 'eslice', 0, 0, tiled=True)  44.3 us
    pallas_call x6, Pallas kernels, call(): pl.pallas_call(kernel, out_shape=tuple(outs), in_specs=[pl.BlockSpec(memo...  42 us
    reduce_scatter x1, waiting for transfers between devices, per_device(): reduced = lax.psum_scatter(grads, 'dp', scatter_dimension=0, tiled=False)  15.5 us
  transfers between devices with their start and end apart: 6, of which 6 were waited for; matrix products, arithmetic and copies ran while one was open for 0% of the time, Pallas kernels for 7%

profile of v1, /device:TPU:1, one launch (start us, length us, event | category | flops | bytes accessed | tf_op | source)
XLA Modules:
  0.0 196.2 jit_solution(17224816738919988328)
XLA Ops:
  7.2 0.0 all-gather.3.cloned.1.call-start
  7.2 3.3 %collective-permute-start = (bf16[2,256,256]{2,1,0:T(8,128)(2,1)}, bf16[2,256,256]{2,1,0:T(8,128)(2,1)S(1)}, u32[]{:S(2)}, u32[]{:S(2)}) collective-permute-start(bf16[2,256,256]{2,1,0:T(8,128)(2,1)} %refs_0_.1), channel_id=1, source_target_pairs={{0,1},{1,0},{2,3},{3,2},{4,5},{5,4},{6,7},{7,6},{8,9},{9,8},{10,11... | collective-permute-start | bytes 786440 | tf_op jit(solution)/shard_map/ppermute | solution.py:266
  10.5 0.1 collective-permute-start.1
  10.6 0.4 collective-permute-start.2
  11.1 0.9 collective-permute-done.refs_3_
  11.9 0.0 copy-start.1
  11.9 0.4 collective-permute-done.1.refs_4_
  12.3 0.0 copy-start.2
  12.3 0.4 collective-permute-done.2.refs_5_
  12.7 0.0 copy-start.3
  12.7 0.0 copy-done.1
  12.7 0.3 copy-done.2
  13.0 0.4 copy-done.3
  13.4 2.3 %pack.1 = bf16[2,3,256,256]{3,2,1,0:T(8,128)(2,1)} custom-call(s32[1]{0:T(128)} %bitcast.3.core_ref, bf16[2,256,256]{2,1,0:T(8,128)(2,1)} %refs_0_.1, bf16[2,256,256]{2,1,0:T(8,128)(2,1)} %refs_1_.1, bf16[2,256,256]{2,1,0:T(8,128)(2,1)} %refs_2_.1, bf16[2,256,256]{2,1,0:T(8,128)(2,1)} %copy-done.1, bf16[2,256,256]{2,1,0:T(8,128)(2,1)} %copy-done.2, ...), custom_call_target="tpu_custom_call" | custom-call | bytes 2097152 | tf_op jit(solution)/shard_map/pack/pallas_call | solution.py:246
  15.7 0.0 all-gather.3.cloned.1.call-update
  15.7 0.0 reduce-scatter.2.cloned.1.call-start
  15.7 5.1 %send.1 = bf16[8,2,2,320,256]{4,3,2,1,0:T(8,128)(2,1)} custom-call(s32[2,128]{1,0:T(2,128)} %bitcast.10, bf16[2,128]{1,0:T(2,128)(2,1)} %bitcast.12, bf16[128,2048]{1,0:T(8,128)(2,1)} %x_ref.1, bf16[128,2048]{1,0:T(8,128)(2,1)} %dy_ref.1), custom_call_target="tpu_custom_call" | custom-call | flops 1000000000 | bytes 6291456 | tf_op jit(solution)/shard_map/send/pallas_call | solution.py:246
  20.8 67.7 %all_to_all.10.rows_in = bf16[32,320,256]{2,1,0:T(8,128)(2,1)} all-to-all(bf16[32,320,256]{2,1,0:T(8,128)(2,1)} %bitcast.7), channel_id=1, replica_groups=mesh['dp'=8,'eslice'=32] {'eslice'}, dimensions={0} | all-to-all | bytes 10485760 | tf_op jit(solution)/shard_map/all_to_all | solution.py:273
  88.5 2.7 %all-gather.3.cloned.1.call-done = bf16[16,3,256,256]{3,2,1,0:T(8,128)(2,1)} async-done(((bf16[2,3,256,256]{3,2,1,0:T(8,128)(2,1)}), bf16[16,3,256,256]{3,2,1,0:T(8,128)(2,1)}) %all-gather.3.cloned.1.call-update) | async-done | bytes 6291472 | tf_op jit(solution)/shard_map/all_gather | solution.py:269
  91.3 18.3 %main.1 = (bf16[2,640,256]{2,1,0:T(8,128)(2,1)}, bf16[2,640,256]{2,1,0:T(8,128)(2,1)}, f32[640,128]{1,0:T(8,128)}, bf16[8,2,3,256,256]{4,3,2,1,0:T(8,128)(2,1)}) custom-call(bf16[32,320,256]{2,1,0:T(8,128)(2,1)} %all_to_all.10.rows_in, bf16[8,2,3,256,256]{4,3,2,1,0:T(8,128)(2,1)} %bitcast.14), custom_call_target="tpu_custom_call" | custom-call | flops 8000000000 | bytes 25165824 | tf_op jit(solution)/shard_map/main/pallas_call | solution.py:246
  109.5 0.0 reduce-scatter.2.cloned.1.call-update
  109.6 10.2 %back.1 = bf16[32,176,256]{2,1,0:T(8,128)(2,1)} custom-call(bf16[2,640,256]{2,1,0:T(8,128)(2,1)} %get-tuple-element.17.dgate_ref, bf16[2,640,256]{2,1,0:T(8,128)(2,1)} %get-tuple-element.18.dup_ref, f32[640,128]{1,0:T(8,128)} %get-tuple-element.19.gate_ref, bf16[8,2,3,256,256]{4,3,2,1,0:T(8,128)(2,1)} %bitcast.15), custom_call_target="tpu_custom_call" | custom-call | flops 3000000000 | bytes 12582912 | tf_op jit(solution)/shard_map/back/pallas_call | solution.py:246
  119.8 44.3 %all_to_all.11.back_ref = bf16[32,176,256]{2,1,0:T(8,128)(2,1)} all-to-all(bf16[32,176,256]{2,1,0:T(8,128)(2,1)} %back.1), channel_id=1, replica_groups=mesh['dp'=8,'eslice'=32] {'eslice'}, dimensions={0} | all-to-all | bytes 5767168 | tf_op jit(solution)/shard_map/all_to_all | solution.py:290
  164.1 3.9 %combine.1 = (bf16[128,2048]{1,0:T(8,128)(2,1)}, f32[2,128]{1,0:T(2,128)}) custom-call(s32[2,128]{1,0:T(2,128)} %bitcast.11, bf16[2,128]{1,0:T(2,128)(2,1)} %bitcast.13, bf16[32,176,256]{2,1,0:T(8,128)(2,1)} %all_to_all.11.back_ref), custom_call_target="tpu_custom_call" | custom-call | flops 1000000000 | bytes 4194304 | tf_op jit(solution)/shard_map/combine/pallas_call | solution.py:246
  168.0 15.5 %reduce-scatter.2.cloned.1.call-done = bf16[1,2,3,256,256]{4,3,2,1,0:T(8,128)(2,1)} async-done(((bf16[8,2,3,256,256]{4,3,2,1,0:T(8,128)(2,1)}), bf16[1,2,3,256,256]{4,3,2,1,0:T(8,128)(2,1)}) %reduce-scatter.2.cloned.1.call-update) | async-done | bytes 786448 | tf_op jit(solution)/shard_map/reduce_scatter | solution.py:284
  183.5 0.6 collective-permute-start.3
  184.1 2.1 %collective-permute-done.3.came_ref = bf16[2,3,256,256]{3,2,1,0:T(8,128)(2,1)S(1)} collective-permute-done((bf16[2,3,256,256]{3,2,1,0:T(8,128)(2,1)}, bf16[2,3,256,256]{3,2,1,0:T(8,128)(2,1)S(1)}, u32[]{:S(2)}, u32[]{:S(2)}) %collective-permute-start.3) | collective-permute-done | bytes 786464 | tf_op jit(solution)/shard_map/ppermute | solution.py:295
  186.2 0.0 copy-start
  186.2 0.9 copy-done
  187.1 2.3 %finish.1 = (bf16[2,256,256]{2,1,0:T(8,128)(2,1)}, bf16[2,256,256]{2,1,0:T(8,128)(2,1)}, bf16[2,256,256]{2,1,0:T(8,128)(2,1)}) custom-call(s32[1]{0:T(128)} %bitcast.3.core_ref, bf16[2,3,256,256]{3,2,1,0:T(8,128)(2,1)} %bitcast.9, bf16[2,3,256,256]{3,2,1,0:T(8,128)(2,1)} %copy-done), custom_call_target="tpu_custom_call" | custom-call | flops 1000000 | bytes 3145728 | tf_op jit(solution)/shard_map/finish/pallas_call | solution.py:246
Async XLA Ops:
  7.2 84.1 %all-gather.3.cloned.1.call-start = ((), (), s32[]{:S(2)}) async-start(), calls=%async_computation.4 | async-start | bytes 7077888 | tf_op jit(solution)/shard_map/all_gather | solution.py:269
  7.2 4.7 %collective-permute-start = (bf16[2,256,256]{2,1,0:T(8,128)(2,1)}, bf16[2,256,256]{2,1,0:T(8,128)(2,1)S(1)}, u32[]{:S(2)}, u32[]{:S(2)}) collective-permute-start(bf16[2,256,256]{2,1,0:T(8,128)(2,1)} %refs_0_.1), channel_id=1, source_target_pairs={{0,1},{1,0},{2,3},{3,2},{4,5},{5,4},{6,7},{7,6},{8,9},{9,8},{10,11... | collective-permute-start | bytes 786440 | tf_op jit(solution)/shard_map/ppermute | solution.py:266
  10.5 1.7 collective-permute-start.1
  10.6 2.0 %collective-permute-start.2 = (bf16[2,256,256]{2,1,0:T(8,128)(2,1)}, bf16[2,256,256]{2,1,0:T(8,128)(2,1)S(1)}, u32[]{:S(2)}, u32[]{:S(2)}) collective-permute-start(bf16[2,256,256]{2,1,0:T(8,128)(2,1)} %refs_2_.1), channel_id=1, source_target_pairs={{0,1},{1,0},{2,3},{3,2},{4,5},{5,4},{6,7},{7,6},{8,9},{9,8},{10,11... | collective-permute-start | bytes 786440 | tf_op jit(solution)/shard_map/ppermute | solution.py:266
  11.9 0.8 copy-start.1
  12.3 0.7 copy-start.2
  12.7 0.7 copy-start.3
  15.7 167.8 %reduce-scatter.2.cloned.1.call-start = ((), (), s32[]{:S(2)}) async-start(), calls=%async_computation.3 | async-start | bytes 7077888 | tf_op jit(solution)/shard_map/reduce_scatter | solution.py:284
  183.5 2.7 %collective-permute-start.3 = (bf16[2,3,256,256]{3,2,1,0:T(8,128)(2,1)}, bf16[2,3,256,256]{3,2,1,0:T(8,128)(2,1)S(1)}, u32[]{:S(2)}, u32[]{:S(2)}) collective-permute-start(bf16[2,3,256,256]{3,2,1,0:T(8,128)(2,1)} %bitcast.8), channel_id=1, source_target_pairs={{0,1},{1,0},{2,3},{3,2},{4,5},{5,4},{6,7},{7,6},{8,9},{9,8},{10,11... | collective-permute-start | bytes 2359304 | tf_op jit(solution)/shard_map/ppermute | solution.py:295
  186.2 0.9 copy-start
Sparse Core Ops, SparseCore 0:
  15.8 75.4 all-gather.2
  109.7 73.7 reduce-scatter.1

commit v2 on v1

--- a/solution.py
+++ b/solution.py
@@ -39,7 +39,7 @@
     return first, second, jnp.where(member, position, -1.0)
 
 
-def send_kernel(routes_ref, gates_ref, x_ref, dy_ref, out_ref):
+def send_kernel(routes_ref, gates_ref, x_ref, dy_ref, out_ref, made_ref, sem):
     first, second, slot = slots(routes_ref[...])
     gates = gates_ref[...].astype(F32)
     gate = jnp.where(first, gates[0:1, :], 0.0) + jnp.where(second, gates[1:2, :], 0.0)
@@ -52,23 +52,30 @@
     rest = slot_row == (row % REST + MAIN).astype(F32)
     block = row // REST % 4
 
-    def put(at, rows):
-        rows = rows.astype(BF).reshape(E // 2, 2, MAIN, CB)
-        for side in range(2):
-            out_ref[:, side, :, at * MAIN:(at + 1) * MAIN, :] = rows
-
-    for base, values, src_ref in ((0, 1.0, x_ref), (10, gate_row, dy_ref)):
+    outs = []
+    for which, (values, src_ref) in enumerate(((1.0, x_ref), (gate_row, dy_ref))):
         pick = jnp.where(main, values, 0.0).astype(BF)
         picks = [jnp.where(jnp.logical_and(rest, block == k), values, 0.0).astype(BF) for k in range(4)]
+        made = made_ref.at[which]
+
+        def put(at, rows):
+            made[:, :, at * MAIN:(at + 1) * MAIN, :] = rows.astype(BF).reshape(E // 2, 2, MAIN, CB)
+
         for group in range(2):
             left = None
             for k in range(4):
                 d = group * 4 + k
                 cols = src_ref[:, d * CB:(d + 1) * CB]
-                put(base + d, dot(pick, cols))
+                put(d, dot(pick, cols))
                 more = dot(picks[k], cols)
                 left = more if left is None else left + more
-            put(base + 8 + group, left)
+            put(8 + group, left)
+        for side in range(2):
+            place = out_ref.at[:, side, :, pl.ds(which * 10 * MAIN, 10 * MAIN), :]
+            outs.append(pltpu.make_async_copy(made, place, sem.at[which, side]))
+            outs[-1].start()
+    for copy in outs:
+        copy.wait()
 
 
 def rest_pick(k):
@@ -79,8 +86,17 @@
 
 
 def pack_kernel(core_ref, *refs):
-    for i, ref in enumerate(refs[:6]):
-        refs[6][i // 3, i % 3] = ref[core_ref[0]]
+    ins, out_ref, held, in_sem, out_sem = refs[:6], *refs[6:]
+    copies = [(pltpu.make_async_copy(ref.at[core_ref[0]], held.at[i // 3, i % 3], in_sem.at[i]),
+               pltpu.make_async_copy(held.at[i // 3, i % 3], out_ref.at[i // 3, i % 3], out_sem.at[i]))
+              for i, ref in enumerate(ins)]
+    for fetch, _ in copies:
+        fetch.start()
+    for fetch, place in copies:
+        fetch.wait()
+        place.start()
+    for _, place in copies:
+        place.wait()
 
 
 def unpack(rows_in, base, into, left_ref, sem):
@@ -102,9 +118,13 @@
         into[SRC:ROWS // MAIN, :, d * CB:(d + 1) * CB] = got.reshape(ROWS // MAIN - SRC, MAIN, CB)
 
 
-def main_kernel(rows_in, w_in, dgate_out, dup_out, gate_out, grad_out,
+def grad_block(rows_ref, side_ref, cols):
+    return dot(rows_ref[:, :, cols].reshape(ROWS, CB), side_ref[...], 0, 0).astype(BF)
+
+
+def main_kernel(rows_in, w_in, side_out, gate_out, grad_out,
                 x_ref, dy_ref, left_ref, w_ref, grad_ref, side_ref, pre_ref, gate_ref,
-                x_sem, dy_sem, w_sem, out_sem, side_sem, gate_sem):
+                x_sem, dy_sem, w_sem, out_sem, end_sem):
     x_copies = unpack(rows_in, 0, x_ref, left_ref.at[0], x_sem)
     dy_copies = unpack(rows_in, 10, dy_ref, left_ref.at[1], dy_sem)
     w_copies = [[[pltpu.make_async_copy(w_in.at[d, q, m], w_ref.at[q, m, d], w_sem.at[q, m, d])
@@ -118,7 +138,6 @@
         for copy in batch:
             copy.start()
     picks = [rest_pick(k) for k in range(4)]
-    outs = []
     for q in range(2):
         for copy in batches[q]:
             copy.wait()
@@ -136,62 +155,83 @@
         sig = jax.nn.sigmoid(gpre)
         act = gpre * sig
         hidden = (act * upre).astype(BF)
-        side_ref[q, 2] = hidden
         part = jnp.sum(hidden.astype(F32) * zeta, axis=1, keepdims=True)
         part = jnp.broadcast_to(part, (ROWS, 128))
         gate_ref[...] = part if q == 0 else gate_ref[...] + part
         side_ref[q, 0] = (zeta * upre * sig * (1.0 + gpre * (1.0 - sig))).astype(BF)
         side_ref[q, 1] = (zeta * act).astype(BF)
-        for d in range(8):
-            for m, rows_ref in enumerate((x_ref, x_ref, dy_ref)):
-                cols = rows_ref[:, :, d * CB:(d + 1) * CB].reshape(ROWS, CB)
-                grad_ref[d, q, m] = dot(cols, side_ref[q, m], 0, 0).astype(BF)
-            if d % 4 == 3:
-                for done in range(d - 3, d + 1):
-                    outs.append(pltpu.make_async_copy(
-                        grad_ref.at[done, q], grad_out.at[done, q], out_sem.at[done, q]))
-                    outs[-1].start()
-            if d == 3:
-                for m, out in enumerate((dgate_out, dup_out)):
-                    outs.append(pltpu.make_async_copy(side_ref.at[q, m], out.at[q], side_sem.at[q, m]))
-                    outs[-1].start()
-    outs.append(pltpu.make_async_copy(gate_ref, gate_out, gate_sem.at[0]))
-    outs[-1].start()
+        side_ref[q, 2] = hidden
+    rows_refs = (x_ref, x_ref, dy_ref)
+    outs = [pltpu.make_async_copy(gate_ref, gate_out, end_sem.at[0]),
+            pltpu.make_async_copy(side_ref.at[:, pl.ds(0, 2)], side_out, end_sem.at[1])]
+    for d in range(8):
+        cols = slice(d * CB, (d + 1) * CB)
+        for q in range(2):
+            for m in range(3):
+                grad_ref[d, q, m] = grad_block(rows_refs[m], side_ref.at[q, m], cols)
+        outs.append(pltpu.make_async_copy(grad_ref.at[d], grad_out.at[d], out_sem.at[d]))
+        if d % 2 == 1:
+            for copy in outs[-2:] if d > 1 else outs:
+                copy.start()
     for copy in outs:
         copy.wait()
 
 
-def back_kernel(dgate_ref, dup_ref, gate_ref, w_in, out_ref, left_ref, w_ref, w_sem):
-    copies = [pltpu.make_async_copy(w_in.at[:, q, m], w_ref.at[q, m], w_sem.at[q, m])
-              for q in range(2) for m in range(2)]
-    for copy in copies:
+def back_kernel(w_in, side_in, gate_in, back_out, w_ref, side_ref, gate_ref, back_ref, w_sem, end_sem):
+    first = [pltpu.make_async_copy(side_in, side_ref, end_sem.at[0]),
+             pltpu.make_async_copy(gate_in, gate_ref, end_sem.at[1])]
+    w_copies = [[pltpu.make_async_copy(w_in.at[d, q, m], w_ref.at[q, m, d], w_sem.at[q, m, d])
+                 for q in range(2) for m in range(2)] for d in range(8)]
+    for copy in first + [copy for copies in w_copies for copy in copies]:
         copy.start()
-    for copy in copies:
-        copy.wait()
     picks = [rest_pick(k) for k in range(4)]
+    for copy in first:
+        copy.wait()
+    outs = []
+
+    def put(at):
+        rows = (slice(None), pl.ds(at * MAIN, MAIN))
+        outs.append(pltpu.make_async_copy(back_ref.at[rows], back_out.at[rows], end_sem.at[2 + at]))
+        outs[-1].start()
+
+    gates = gate_ref[...].astype(BF)
+    back_ref[:, 10 * MAIN:11 * MAIN, 0:128] = gates[0:FULL].reshape(SRC, MAIN, 128)
+    spread = dot(picks[0], gates[FULL:ROWS], 0, 0).astype(BF)
+    back_ref[:, 10 * MAIN:11 * MAIN, 128:256] = spread.reshape(SRC, MAIN, 128)
+    put(10)
     for group in range(2):
         left = None
+        for copies in w_copies[group * 4:group * 4 + 4]:
+            for copy in copies:
+                copy.wait()
         for k in range(4):
             d = group * 4 + k
-            total = dot(dgate_ref[0], w_ref[0, 0, d], 1, 1) + dot(dup_ref[0], w_ref[0, 1, d], 1, 1)
-            total += dot(dgate_ref[1], w_ref[1, 0, d], 1, 1) + dot(dup_ref[1], w_ref[1, 1, d], 1, 1)
+            total = dot(side_ref[0, 0], w_ref[0, 0, d], 1, 1) + dot(side_ref[0, 1], w_ref[0, 1, d], 1, 1)
+            total += dot(side_ref[1, 0], w_ref[1, 0, d], 1, 1) + dot(side_ref[1, 1], w_ref[1, 1, d], 1, 1)
             rows = total.astype(BF)
-            out_ref[:, d * MAIN:(d + 1) * MAIN, :] = rows[0:FULL].reshape(SRC, MAIN, CB)
+            back_ref[:, d * MAIN:(d + 1) * MAIN, :] = rows[0:FULL].reshape(SRC, MAIN, CB)
             more = dot(picks[k], rows[FULL:ROWS], 0, 0)
             left = more if left is None else left + more
-        at = (8 + group) * MAIN
-        out_ref[:, at:at + MAIN, :] = left.astype(BF).reshape(SRC, MAIN, CB)
-    gates = gate_ref[...].astype(BF)
-    out_ref[:, 10 * MAIN:11 * MAIN, 0:128] = gates[0:FULL].reshape(SRC, MAIN, 128)
-    spread = dot(picks[0], gates[FULL:ROWS], 0, 0).astype(BF)
-    out_ref[:, 10 * MAIN:11 * MAIN, 128:256] = spread.reshape(SRC, MAIN, 128)
-
-
-def finish_kernel(core_ref, kept_ref, came_ref, *out_refs):
+        back_ref[:, (8 + group) * MAIN:(9 + group) * MAIN, :] = left.astype(BF).reshape(SRC, MAIN, CB)
+        for at in (*range(group * 4, group * 4 + 4), 8 + group):
+            put(at)
+    for copy in outs:
+        copy.wait()
+
+
+def finish_kernel(core_ref, own_ref, came_ref, *refs):
+    outs, (held, in_sem, out_sem) = refs[:3], refs[3:]
     core = core_ref[0]
-    for m, out_ref in enumerate(out_refs):
-        out_ref[core] = kept_ref[0, m]
-        out_ref[1 - core] = came_ref[1, m]
+    fetches = [pltpu.make_async_copy(own_ref.at[0, m], held.at[m], in_sem.at[m]) for m in range(3)]
+    places = [pltpu.make_async_copy(held.at[m], outs[m].at[core], out_sem.at[m]) for m in range(3)]
+    came = [pltpu.make_async_copy(came_ref.at[1, m], outs[m].at[1 - core], out_sem.at[3 + m]) for m in range(3)]
+    for copy in fetches + came:
+        copy.start()
+    for fetch, place in zip(fetches, places):
+        fetch.wait()
+        place.start()
+    for copy in came + places:
+        copy.wait()
 
 
 def combine_kernel(routes_ref, gates_ref, back_ref, grad_ref, gate_ref):
@@ -227,10 +267,6 @@
     return [pl.BlockSpec(memory_space=pltpu.VMEM)] * count
 
 
-def params():
-    return pltpu.CompilerParams(vmem_limit_bytes=60 * MB)
-
-
 def cost(flops, moved):
     return pl.CostEstimate(flops=flops, bytes_accessed=moved, transcendentals=0)
 
@@ -239,7 +275,7 @@
     return jax.ShapeDtypeStruct(sizes, dtype)
 
 
-def call(kernel, name, outs, args, flops, moved, kinds=None, out_kinds=None, scratch=()):
+def call(kernel, name, outs, args, flops, moved, kinds=None, out_kinds=None, scratch=(), limit=63400000):
     spaces = {"s": pltpu.SMEM, "v": pltpu.VMEM, "a": pl.ANY}
     kinds = kinds or "v" * len(args)
     out_kinds = out_kinds or "v" * len(outs)
@@ -249,7 +285,7 @@
         in_specs=[pl.BlockSpec(memory_space=spaces[k]) for k in kinds],
         out_specs=tuple(pl.BlockSpec(memory_space=spaces[k]) for k in out_kinds),
         scratch_shapes=list(scratch),
-        compiler_params=params(),
+        compiler_params=pltpu.CompilerParams(vmem_limit_bytes=limit),
         cost_estimate=cost(flops, moved),
         name=name,
     )(*args)
@@ -265,36 +301,41 @@
 
     theirs = [lax.ppermute(w, "eslice", PARTNER) for w in mats]
     (packed,) = call(pack_kernel, "pack", [shape(2, 3, CB, CB)], (core, *mats, *theirs), 0, 2 * MB,
-                     kinds="svvvvvv")
+                     kinds="saaaaaa", out_kinds="a",
+                     scratch=(pltpu.VMEM((2, 3, CB, CB), BF), dma((6,)), dma((6,))))
     weights = lax.all_gather(packed, "dp", axis=0, tiled=False)
 
     (sent,) = call(send_kernel, "send", [shape(E // 2, 2, 2, 20 * MAIN, CB)],
-                   (routes.T, gate_weights.T, inputs, cotangent), 10**9, 6 * MB)
+                   (routes.T, gate_weights.T, inputs, cotangent), 10**9, 6 * MB, kinds="vvvv", out_kinds="a",
+                   scratch=(pltpu.VMEM((2, E // 2, 2, 10 * MAIN, CB), BF), dma((2, 2))))
     rows = lax.all_to_all(sent.reshape(SRC, 20 * MAIN, CB), "eslice", 0, 0, tiled=True)
 
     tiles = pltpu.VMEM((ROWS // MAIN, MAIN, D), BF)
-    dgate, dup, gate_part, grads = call(
+    rests = pltpu.VMEM((2, 2, SRC, MAIN, CB), BF)
+    gate_vmem = pltpu.VMEM((ROWS, 128), F32)
+    side, gate_part, grads = call(
         main_kernel, "main",
-        [shape(2, ROWS, CB), shape(2, ROWS, CB), shape(ROWS, 128, dtype=F32), shape(8, 2, 3, CB, CB)],
-        (rows, weights), 8 * 10**9, 24 * MB, kinds="aa", out_kinds="aaaa",
-        scratch=(tiles, tiles, pltpu.VMEM((2, 2, SRC, MAIN, CB), BF), pltpu.VMEM((2, 3, 8, CB, CB), BF),
+        [shape(2, 2, ROWS, CB), shape(ROWS, 128, dtype=F32), shape(8, 2, 3, CB, CB)],
+        (rows, weights), 8 * 10**9, 24 * MB, kinds="aa", out_kinds="aaa",
+        scratch=(tiles, tiles, rests, pltpu.VMEM((2, 3, 8, CB, CB), BF),
                  pltpu.VMEM((8, 2, 3, CB, CB), BF), pltpu.VMEM((2, 3, ROWS, CB), BF),
-                 pltpu.VMEM((2, 2, ROWS, CB), F32), pltpu.VMEM((ROWS, 128), F32),
-                 dma((10,)), dma((10,)), dma((2, 3, 8)), dma((8, 2)), dma((2, 2)), dma((1,))))
+                 pltpu.VMEM((2, 2, ROWS, CB), F32), gate_vmem,
+                 dma((10,)), dma((10,)), dma((2, 3, 8)), dma((8,)), dma((2,))))
     reduced = lax.psum_scatter(grads, "dp", scatter_dimension=0, tiled=False)
 
     (back,) = call(
-        back_kernel, "back", [shape(SRC, 11 * MAIN, CB)], (dgate, dup, gate_part, weights),
-        3 * 10**9, 12 * MB, kinds="vvva",
-        scratch=(pltpu.VMEM((2, FULL, CB), F32), pltpu.VMEM((2, 2, 8, CB, CB), BF), dma((2, 2))))
+        back_kernel, "back", [shape(SRC, 11 * MAIN, CB)], (weights, side, gate_part), 3 * 10**9, 10 * MB,
+        kinds="aaa", out_kinds="a",
+        scratch=(pltpu.VMEM((2, 2, 8, CB, CB), BF), pltpu.VMEM((2, 2, ROWS, CB), BF), gate_vmem,
+                 pltpu.VMEM((SRC, 11 * MAIN, CB), BF), dma((2, 2, 8)), dma((13,))))
     returned = lax.all_to_all(back, "eslice", 0, 0, tiled=True)
     input_grad, gate_grad = call(combine_kernel, "combine", [shape(T, D), shape(2, T, dtype=F32)],
                                  (routes.T, gate_weights.T, returned), 10**9, 4 * MB)
-
     reduced, input_grad = lax.optimization_barrier((reduced, input_grad))
     came = lax.ppermute(reduced, "eslice", PARTNER)
-    grads = call(finish_kernel, "finish", [shape(2, CB, CB)] * 3,
-                 (core, reduced, came), 10**6, 3 * MB, kinds="svv")
+    grads = call(finish_kernel, "finish", [shape(2, CB, CB)] * 3, (core, reduced, came), 10**6, 3 * MB,
+                 kinds="sav", out_kinds="aaa", limit=4 * MB,
+                 scratch=(pltpu.VMEM((3, CB, CB), BF), dma((3,)), dma((6,))))
     return (input_grad, gate_grad.T, *grads)
 
 

time: 197 us -> 193 us (0.980)
  Pallas kernels: 42 us -> 37.8 us
    pallas_call x6, Pallas kernels: 42 us -> 37.8 us  [call(): pl.pallas_call(kernel, out_shape=tuple(outs), in_specs=[pl.BlockSpec(memo...]
where the time goes in v2:
time: 193 us
  blocking collectives  112 us (58%)
  Pallas kernels  37.8 us (20%)
  waiting for transfers between devices  22.8 us (12%)
  between operations  14.1 us (7%)
  starting transfers between devices  4.54 us (2%)
    all_to_all x1, blocking collectives, per_device(): lax.all_to_all(sent.reshape(SRC, 20 * MAIN, CB), 'eslice', 0, 0, tiled=True)  67.7 us
    all_to_all x1, blocking collectives, per_device(): returned = lax.all_to_all(back, 'eslice', 0, 0, tiled=True)  44.3 us
    pallas_call x6, Pallas kernels, call(): pl.pallas_call(kernel, out_shape=tuple(outs), in_specs=[pl.BlockSpec(memo...  37.8 us
    reduce_scatter x1, waiting for transfers between devices, per_device(): reduced = lax.psum_scatter(grads, 'dp', scatter_dimension=0, tiled=False)  15.9 us
  transfers between devices with their start and end apart: 6, of which 6 were waited for; matrix products, arithmetic and copies ran while one was open for 0% of the time, Pallas kernels for 7%

profile of v2, /device:TPU:1, one launch (start us, length us, event | category | flops | bytes accessed | tf_op | source)
XLA Modules:
  0.0 193.1 jit_solution(17141266459983970168)
XLA Ops:
  7.2 0.0 all-gather.3.cloned.1.call-start
  7.2 3.3 %collective-permute-start = (bf16[2,256,256]{2,1,0:T(8,128)(2,1)}, bf16[2,256,256]{2,1,0:T(8,128)(2,1)S(1)}, u32[]{:S(2)}, u32[]{:S(2)}) collective-permute-start(bf16[2,256,256]{2,1,0:T(8,128)(2,1)} %refs_0_.1), channel_id=1, source_target_pairs={{0,1},{1,0},{2,3},{3,2},{4,5},{5,4},{6,7},{7,6},{8,9},{9,8},{10,11... | collective-permute-start | bytes 786440 | tf_op jit(solution)/shard_map/ppermute | solution.py:302
  10.5 0.1 collective-permute-start.1
  10.6 0.4 collective-permute-start.2
  11.1 0.9 collective-permute-done.refs_3_
  11.9 0.0 copy-start.1
  11.9 0.4 collective-permute-done.1.refs_4_
  12.3 0.0 copy-start.2
  12.3 0.4 collective-permute-done.2.refs_5_
  12.7 0.0 copy-start.3
  12.7 0.0 copy-done.1
  12.7 0.3 copy-done.2
  13.0 0.4 copy-done.3
  13.4 2.0 %pack.1 = bf16[2,3,256,256]{3,2,1,0:T(8,128)(2,1)} custom-call(s32[1]{0:T(128)} %bitcast.3.core_ref, bf16[2,256,256]{2,1,0:T(8,128)(2,1)} %refs_0_.1, bf16[2,256,256]{2,1,0:T(8,128)(2,1)} %refs_1_.1, bf16[2,256,256]{2,1,0:T(8,128)(2,1)} %refs_2_.1, bf16[2,256,256]{2,1,0:T(8,128)(2,1)} %copy-done.1, bf16[2,256,256]{2,1,0:T(8,128)(2,1)} %copy-done.2, ...), custom_call_target="tpu_custom_call" | custom-call | bytes 2097152 | tf_op jit(solution)/shard_map/pack/pallas_call | solution.py:282
  15.4 0.0 all-gather.3.cloned.1.call-update
  15.4 0.0 reduce-scatter.2.cloned.1.call-start
  15.4 4.7 %send.1 = bf16[8,2,2,320,256]{4,3,2,1,0:T(8,128)(2,1)} custom-call(s32[2,128]{1,0:T(2,128)} %bitcast.10, bf16[2,128]{1,0:T(2,128)(2,1)} %bitcast.12, bf16[128,2048]{1,0:T(8,128)(2,1)} %x_ref.1, bf16[128,2048]{1,0:T(8,128)(2,1)} %dy_ref.1), custom_call_target="tpu_custom_call" | custom-call | flops 1000000000 | bytes 6291456 | tf_op jit(solution)/shard_map/send/pallas_call | solution.py:282
  20.1 67.7 %all_to_all.10.rows_in = bf16[32,320,256]{2,1,0:T(8,128)(2,1)} all-to-all(bf16[32,320,256]{2,1,0:T(8,128)(2,1)} %bitcast.9), channel_id=1, replica_groups=mesh['dp'=8,'eslice'=32] {'eslice'}, dimensions={0} | all-to-all | bytes 10485760 | tf_op jit(solution)/shard_map/all_to_all | solution.py:311
  87.8 3.2 %all-gather.3.cloned.1.call-done = bf16[16,3,256,256]{3,2,1,0:T(8,128)(2,1)} async-done(((bf16[2,3,256,256]{3,2,1,0:T(8,128)(2,1)}), bf16[16,3,256,256]{3,2,1,0:T(8,128)(2,1)}) %all-gather.3.cloned.1.call-update) | async-done | bytes 6291472 | tf_op jit(solution)/shard_map/all_gather | solution.py:306
  91.0 16.1 %main.1 = (bf16[2,2,640,256]{3,2,1,0:T(8,128)(2,1)}, f32[640,128]{1,0:T(8,128)}, bf16[8,2,3,256,256]{4,3,2,1,0:T(8,128)(2,1)}) custom-call(bf16[32,320,256]{2,1,0:T(8,128)(2,1)} %all_to_all.10.rows_in, bf16[8,2,3,256,256]{4,3,2,1,0:T(8,128)(2,1)} %bitcast.14), custom_call_target="tpu_custom_call" | custom-call | flops 8000000000 | bytes 25165824 | tf_op jit(solution)/shard_map/main/pallas_call | solution.py:282
  107.0 0.0 reduce-scatter.2.cloned.1.call-update
  107.1 9.8 %back.1 = bf16[32,176,256]{2,1,0:T(8,128)(2,1)} custom-call(bf16[8,2,3,256,256]{4,3,2,1,0:T(8,128)(2,1)} %bitcast.15, bf16[2,2,640,256]{3,2,1,0:T(8,128)(2,1)} %get-tuple-element.16.side_in, f32[640,128]{1,0:T(8,128)} %get-tuple-element.17.gate_in), custom_call_target="tpu_custom_call" | custom-call | flops 3000000000 | bytes 10485760 | tf_op jit(solution)/shard_map/back/pallas_call | solution.py:282
  116.8 44.3 %all_to_all.11.back_ref = bf16[32,176,256]{2,1,0:T(8,128)(2,1)} all-to-all(bf16[32,176,256]{2,1,0:T(8,128)(2,1)} %back.1), channel_id=1, replica_groups=mesh['dp'=8,'eslice'=32] {'eslice'}, dimensions={0} | all-to-all | bytes 5767168 | tf_op jit(solution)/shard_map/all_to_all | solution.py:331
  161.2 3.9 %combine.1 = (bf16[128,2048]{1,0:T(8,128)(2,1)}, f32[2,128]{1,0:T(2,128)}) custom-call(s32[2,128]{1,0:T(2,128)} %bitcast.11, bf16[2,128]{1,0:T(2,128)(2,1)} %bitcast.13, bf16[32,176,256]{2,1,0:T(8,128)(2,1)} %all_to_all.11.back_ref), custom_call_target="tpu_custom_call" | custom-call | flops 1000000000 | bytes 4194304 | tf_op jit(solution)/shard_map/combine/pallas_call | solution.py:282
  165.1 15.9 %reduce-scatter.2.cloned.1.call-done = bf16[1,2,3,256,256]{4,3,2,1,0:T(8,128)(2,1)} async-done(((bf16[8,2,3,256,256]{4,3,2,1,0:T(8,128)(2,1)}), bf16[1,2,3,256,256]{4,3,2,1,0:T(8,128)(2,1)}) %reduce-scatter.2.cloned.1.call-update) | async-done | bytes 786448 | tf_op jit(solution)/shard_map/reduce_scatter | solution.py:324
  181.0 0.6 collective-permute-start.3
  181.6 2.1 %collective-permute-done.3.came_ref = bf16[2,3,256,256]{3,2,1,0:T(8,128)(2,1)S(1)} collective-permute-done((bf16[2,3,256,256]{3,2,1,0:T(8,128)(2,1)}, bf16[2,3,256,256]{3,2,1,0:T(8,128)(2,1)S(1)}, u32[]{:S(2)}, u32[]{:S(2)}) %collective-permute-start.3) | collective-permute-done | bytes 786464 | tf_op jit(solution)/shard_map/ppermute | solution.py:335
  183.7 0.0 copy-start
  183.7 1.1 copy-done
  184.8 1.4 finish.1
Async XLA Ops:
  7.2 83.8 %all-gather.3.cloned.1.call-start = ((), (), s32[]{:S(2)}) async-start(), calls=%async_computation.4 | async-start | bytes 7077888 | tf_op jit(solution)/shard_map/all_gather | solution.py:306
  7.2 4.7 %collective-permute-start = (bf16[2,256,256]{2,1,0:T(8,128)(2,1)}, bf16[2,256,256]{2,1,0:T(8,128)(2,1)S(1)}, u32[]{:S(2)}, u32[]{:S(2)}) collective-permute-start(bf16[2,256,256]{2,1,0:T(8,128)(2,1)} %refs_0_.1), channel_id=1, source_target_pairs={{0,1},{1,0},{2,3},{3,2},{4,5},{5,4},{6,7},{7,6},{8,9},{9,8},{10,11... | collective-permute-start | bytes 786440 | tf_op jit(solution)/shard_map/ppermute | solution.py:302
  10.5 1.7 collective-permute-start.1
  10.6 2.0 %collective-permute-start.2 = (bf16[2,256,256]{2,1,0:T(8,128)(2,1)}, bf16[2,256,256]{2,1,0:T(8,128)(2,1)S(1)}, u32[]{:S(2)}, u32[]{:S(2)}) collective-permute-start(bf16[2,256,256]{2,1,0:T(8,128)(2,1)} %refs_2_.1), channel_id=1, source_target_pairs={{0,1},{1,0},{2,3},{3,2},{4,5},{5,4},{6,7},{7,6},{8,9},{9,8},{10,11... | collective-permute-start | bytes 786440 | tf_op jit(solution)/shard_map/ppermute | solution.py:302
  11.9 0.8 copy-start.1
  12.3 0.7 copy-start.2
  12.7 0.7 copy-start.3
  15.4 165.6 %reduce-scatter.2.cloned.1.call-start = ((), (), s32[]{:S(2)}) async-start(), calls=%async_computation.3 | async-start | bytes 7077888 | tf_op jit(solution)/shard_map/reduce_scatter | solution.py:324
  181.0 2.7 %collective-permute-start.3 = (bf16[2,3,256,256]{3,2,1,0:T(8,128)(2,1)}, bf16[2,3,256,256]{3,2,1,0:T(8,128)(2,1)S(1)}, u32[]{:S(2)}, u32[]{:S(2)}) collective-permute-start(bf16[2,3,256,256]{3,2,1,0:T(8,128)(2,1)} %bitcast.7), channel_id=1, source_target_pairs={{0,1},{1,0},{2,3},{3,2},{4,5},{5,4},{6,7},{7,6},{8,9},{9,8},{10,11... | collective-permute-start | bytes 2359304 | tf_op jit(solution)/shard_map/ppermute | solution.py:335
  183.7 1.1 copy-start
Sparse Core Ops, SparseCore 0:
  15.5 75.4 all-gather.2
  107.2 73.7 reduce-scatter.1

commit v3 on v2

--- a/solution.py
+++ b/solution.py
@@ -83,20 +83,6 @@
     r, c = iota(shape, 0), iota(shape, 1)
     hit = jnp.logical_and(r // REST == c // MAIN, r % REST == c % REST)
     return jnp.logical_and(hit, c // REST % 4 == k).astype(F32).astype(BF)
-
-
-def pack_kernel(core_ref, *refs):
-    ins, out_ref, held, in_sem, out_sem = refs[:6], *refs[6:]
-    copies = [(pltpu.make_async_copy(ref.at[core_ref[0]], held.at[i // 3, i % 3], in_sem.at[i]),
-               pltpu.make_async_copy(held.at[i // 3, i % 3], out_ref.at[i // 3, i % 3], out_sem.at[i]))
-              for i, ref in enumerate(ins)]
-    for fetch, _ in copies:
-        fetch.start()
-    for fetch, place in copies:
-        fetch.wait()
-        place.start()
-    for _, place in copies:
-        place.wait()
 
 
 def unpack(rows_in, base, into, left_ref, sem):
@@ -216,21 +202,6 @@
         for at in (*range(group * 4, group * 4 + 4), 8 + group):
             put(at)
     for copy in outs:
-        copy.wait()
-
-
-def finish_kernel(core_ref, own_ref, came_ref, *refs):
-    outs, (held, in_sem, out_sem) = refs[:3], refs[3:]
-    core = core_ref[0]
-    fetches = [pltpu.make_async_copy(own_ref.at[0, m], held.at[m], in_sem.at[m]) for m in range(3)]
-    places = [pltpu.make_async_copy(held.at[m], outs[m].at[core], out_sem.at[m]) for m in range(3)]
-    came = [pltpu.make_async_copy(came_ref.at[1, m], outs[m].at[1 - core], out_sem.at[3 + m]) for m in range(3)]
-    for copy in fetches + came:
-        copy.start()
-    for fetch, place in zip(fetches, places):
-        fetch.wait()
-        place.start()
-    for copy in came + places:
         copy.wait()
 
 
@@ -295,14 +266,13 @@
 
 
 def per_device(inputs, cotangent, routes, gate_weights, gate_weight, up_weight, down_weight):
-    core = (lax.axis_index("eslice") % 2).reshape(1)
+    core = lax.axis_index("eslice") % 2
     dma = pltpu.SemaphoreType.DMA
     mats = (gate_weight, up_weight, down_weight)
 
     theirs = [lax.ppermute(w, "eslice", PARTNER) for w in mats]
-    (packed,) = call(pack_kernel, "pack", [shape(2, 3, CB, CB)], (core, *mats, *theirs), 0, 2 * MB,
-                     kinds="saaaaaa", out_kinds="a",
-                     scratch=(pltpu.VMEM((2, 3, CB, CB), BF), dma((6,)), dma((6,))))
+    second = core == 1
+    packed = jnp.stack([jnp.where(second, w[1], w[0]) for w in (*mats, *theirs)]).reshape(2, 3, CB, CB)
     weights = lax.all_gather(packed, "dp", axis=0, tiled=False)
 
     (sent,) = call(send_kernel, "send", [shape(E // 2, 2, 2, 20 * MAIN, CB)],
@@ -333,9 +303,10 @@
                                  (routes.T, gate_weights.T, returned), 10**9, 4 * MB)
     reduced, input_grad = lax.optimization_barrier((reduced, input_grad))
     came = lax.ppermute(reduced, "eslice", PARTNER)
-    grads = call(finish_kernel, "finish", [shape(2, CB, CB)] * 3, (core, reduced, came), 10**6, 3 * MB,
-                 kinds="sav", out_kinds="aaa", limit=4 * MB,
-                 scratch=(pltpu.VMEM((3, CB, CB), BF), dma((3,)), dma((6,))))
+    grads = []
+    for m in range(3):
+        low, high = (jnp.where(first, reduced[0, m], came[1, m]) for first in (core == 0, second))
+        grads.append(jnp.stack((low, high)))
     return (input_grad, gate_grad.T, *grads)
 
 

time: 193 us -> 193 us (level)
  other arithmetic: 0 us -> 5.77 us
  Pallas kernels: 37.8 us -> 34.4 us
    pallas_call x6 -> x4, Pallas kernels: 37.8 us -> 34.4 us  [call(): pl.pallas_call(kernel, out_shape=tuple(outs), in_specs=[pl.BlockSpec(memo...]
    unnamed x0 -> x5, other arithmetic: none -> 3.08 us
  transfers between devices with their start and end apart: 6 -> 6, of which waited for: 6 -> 3; matrix products, arithmetic and copies ran while one was open for 0% -> 2% of each run, Pallas kernels for 7% -> 7%
where the time goes in v3:
time: 193 us
  blocking collectives  112 us (58%)
  Pallas kernels  34.4 us (18%)
  waiting for transfers between devices  21.3 us (11%)
  between operations  14.1 us (7%)
  other arithmetic  5.77 us (3%)
  starting transfers between devices  4.51 us (2%)
    all_to_all x1, blocking collectives, per_device(): lax.all_to_all(sent.reshape(SRC, 20 * MAIN, CB), 'eslice', 0, 0, tiled=True)  67.5 us
    all_to_all x1, blocking collectives, per_device(): returned = lax.all_to_all(back, 'eslice', 0, 0, tiled=True)  44.3 us
    pallas_call x4, Pallas kernels, call(): pl.pallas_call(kernel, out_shape=tuple(outs), in_specs=[pl.BlockSpec(memo...  34.4 us
    reduce_scatter x1, waiting for transfers between devices, per_device(): reduced = lax.psum_scatter(grads, 'dp', scatter_dimension=0, tiled=False)  15.9 us
  transfers between devices with their start and end apart: 6, of which 3 were waited for; matrix products, arithmetic and copies ran while one was open for 2% of the time, Pallas kernels for 7%

profile of v3, /device:TPU:1, one launch (start us, length us, event | category | flops | bytes accessed | tf_op | source)
XLA Modules:
  0.0 192.7 jit_solution(11010692651579096894)
XLA Ops:
  7.2 0.0 all-gather.2.cloned.1.call-start
  7.2 3.3 %collective-permute-start = (bf16[2,256,256]{2,1,0:T(8,128)(2,1)}, bf16[2,256,256]{2,1,0:T(8,128)(2,1)S(1)}, u32[]{:S(2)}, u32[]{:S(2)}) collective-permute-start(bf16[2,256,256]{2,1,0:T(8,128)(2,1)} %param.11), channel_id=1, source_target_pairs={{0,1},{1,0},{2,3},{3,2},{4,5},{5,4},{6,7},{7,6},{8,9},{9,8},{10,11... | collective-permute-start | bytes 786440 | tf_op jit(solution)/shard_map/ppermute | solution.py:273
  10.5 0.1 collective-permute-start.1
  10.6 0.4 collective-permute-start.2
  11.0 1.0 select_dynamic-update-slice_fusion.2
  12.1 1.0 select_dynamic-update-slice_fusion.1
  13.1 1.0 select_dynamic-update-slice_fusion
  14.1 0.0 collective-permute-done
  14.1 0.0 collective-permute-done.1
  14.2 0.0 collective-permute-done.2
  14.2 0.0 copy-start
  14.2 0.9 copy-done
  15.1 0.0 all-gather.2.cloned.1.call-update
  15.1 0.0 reduce-scatter.2.cloned.1.call-start
  15.2 4.7 %send.1 = bf16[8,2,2,320,256]{4,3,2,1,0:T(8,128)(2,1)} custom-call(s32[2,128]{1,0:T(2,128)} %bitcast.22, bf16[2,128]{1,0:T(2,128)(2,1)} %bitcast.24, bf16[128,2048]{1,0:T(8,128)(2,1)} %x_ref.1, bf16[128,2048]{1,0:T(8,128)(2,1)} %dy_ref.1), custom_call_target="tpu_custom_call" | custom-call | flops 1000000000 | bytes 6291456 | tf_op jit(solution)/shard_map/send/pallas_call | solution.py:253
  19.8 67.5 %all_to_all.10.rows_in = bf16[32,320,256]{2,1,0:T(8,128)(2,1)} all-to-all(bf16[32,320,256]{2,1,0:T(8,128)(2,1)} %bitcast.18), channel_id=1, replica_groups=mesh['dp'=8,'eslice'=32] {'eslice'}, dimensions={0} | all-to-all | bytes 10485760 | tf_op jit(solution)/shard_map/all_to_all | solution.py:281
  87.3 3.2 %all-gather.2.cloned.1.call-done.w_in = bf16[8,2,3,256,256]{4,3,2,1,0:T(8,128)(2,1)} async-done(((bf16[1,2,3,256,256]{4,3,2,1,0:T(8,128)(2,1)}), bf16[8,2,3,256,256]{4,3,2,1,0:T(8,128)(2,1)}) %all-gather.2.cloned.1.call-update) | async-done | bytes 6291472 | tf_op jit(solution)/shard_map/all_gather | solution.py:276
  90.5 16.1 %main.1 = (bf16[2,2,640,256]{3,2,1,0:T(8,128)(2,1)}, f32[640,128]{1,0:T(8,128)}, bf16[8,2,3,256,256]{4,3,2,1,0:T(8,128)(2,1)}) custom-call(bf16[32,320,256]{2,1,0:T(8,128)(2,1)} %all_to_all.10.rows_in, bf16[8,2,3,256,256]{4,3,2,1,0:T(8,128)(2,1)} %all-gather.2.cloned.1.call-done.w_in), custom_call_target="tpu_custom_call" | custom-call | flops 8000000000 | bytes 25165824 | tf_op jit(solution)/shard_map/main/pallas_call | solution.py:253
  106.6 0.0 reduce-scatter.2.cloned.1.call-update
  106.6 9.8 %back.1 = bf16[32,176,256]{2,1,0:T(8,128)(2,1)} custom-call(bf16[8,2,3,256,256]{4,3,2,1,0:T(8,128)(2,1)} %all-gather.2.cloned.1.call-done.w_in, bf16[2,2,640,256]{3,2,1,0:T(8,128)(2,1)} %get-tuple-element.13.side_in, f32[640,128]{1,0:T(8,128)} %get-tuple-element.14.gate_in), custom_call_target="tpu_custom_call" | custom-call | flops 3000000000 | bytes 10485760 | tf_op jit(solution)/shard_map/back/pallas_call | solution.py:253
  116.4 44.3 %all_to_all.11.back_ref = bf16[32,176,256]{2,1,0:T(8,128)(2,1)} all-to-all(bf16[32,176,256]{2,1,0:T(8,128)(2,1)} %back.1), channel_id=1, replica_groups=mesh['dp'=8,'eslice'=32] {'eslice'}, dimensions={0} | all-to-all | bytes 5767168 | tf_op jit(solution)/shard_map/all_to_all | solution.py:301
  160.7 3.9 %combine.1 = (bf16[128,2048]{1,0:T(8,128)(2,1)}, f32[2,128]{1,0:T(2,128)}) custom-call(s32[2,128]{1,0:T(2,128)} %bitcast.23, bf16[2,128]{1,0:T(2,128)(2,1)} %bitcast.25, bf16[32,176,256]{2,1,0:T(8,128)(2,1)} %all_to_all.11.back_ref), custom_call_target="tpu_custom_call" | custom-call | flops 1000000000 | bytes 4194304 | tf_op jit(solution)/shard_map/combine/pallas_call | solution.py:253
  164.6 15.9 %reduce-scatter.2.cloned.1.call-done = bf16[1,2,3,256,256]{4,3,2,1,0:T(8,128)(2,1)} async-done(((bf16[8,2,3,256,256]{4,3,2,1,0:T(8,128)(2,1)}), bf16[1,2,3,256,256]{4,3,2,1,0:T(8,128)(2,1)}) %reduce-scatter.2.cloned.1.call-update) | async-done | bytes 786448 | tf_op jit(solution)/shard_map/reduce_scatter | solution.py:294
  180.5 0.6 collective-permute-start.3
  181.1 2.1 %collective-permute-done.3 = bf16[2,3,256,256]{3,2,1,0:T(8,128)(2,1)S(1)} collective-permute-done((bf16[2,3,256,256]{3,2,1,0:T(8,128)(2,1)}, bf16[2,3,256,256]{3,2,1,0:T(8,128)(2,1)S(1)}, u32[]{:S(2)}, u32[]{:S(2)}) %collective-permute-start.3) | collective-permute-done | bytes 786464 | tf_op jit(solution)/shard_map/ppermute | solution.py:305
  183.2 1.1 select_bitcast_fusion.1
  184.3 0.7 pad_maximum_fusion.2
  185.1 0.8 pad_maximum_fusion
  (3 shorter events, 0.1 us)
Async XLA Ops:
  7.2 83.3 %all-gather.2.cloned.1.call-start = ((), (), s32[]{:S(2)}) async-start(), calls=%async_computation.3 | async-start | bytes 7077888 | tf_op jit(solution)/shard_map/all_gather | solution.py:276
  7.2 6.9 %collective-permute-start = (bf16[2,256,256]{2,1,0:T(8,128)(2,1)}, bf16[2,256,256]{2,1,0:T(8,128)(2,1)S(1)}, u32[]{:S(2)}, u32[]{:S(2)}) collective-permute-start(bf16[2,256,256]{2,1,0:T(8,128)(2,1)} %param.11), channel_id=1, source_target_pairs={{0,1},{1,0},{2,3},{3,2},{4,5},{5,4},{6,7},{7,6},{8,9},{9,8},{10,11... | collective-permute-start | bytes 786440 | tf_op jit(solution)/shard_map/ppermute | solution.py:273
  10.5 3.6 %collective-permute-start.1 = (bf16[2,256,256]{2,1,0:T(8,128)(2,1)}, bf16[2,256,256]{2,1,0:T(8,128)(2,1)S(1)}, u32[]{:S(2)}, u32[]{:S(2)}) collective-permute-start(bf16[2,256,256]{2,1,0:T(8,128)(2,1)} %param.12), channel_id=1, source_target_pairs={{0,1},{1,0},{2,3},{3,2},{4,5},{5,4},{6,7},{7,6},{8,9},{9,8},{10,11... | collective-permute-start | bytes 786440 | tf_op jit(solution)/shard_map/ppermute | solution.py:273
  10.6 3.5 %collective-permute-start.2 = (bf16[2,256,256]{2,1,0:T(8,128)(2,1)}, bf16[2,256,256]{2,1,0:T(8,128)(2,1)S(1)}, u32[]{:S(2)}, u32[]{:S(2)}) collective-permute-start(bf16[2,256,256]{2,1,0:T(8,128)(2,1)} %param.13), channel_id=1, source_target_pairs={{0,1},{1,0},{2,3},{3,2},{4,5},{5,4},{6,7},{7,6},{8,9},{9,8},{10,11... | collective-permute-start | bytes 786440 | tf_op jit(solution)/shard_map/ppermute | solution.py:273
  14.2 0.9 copy-start
  15.1 165.4 %reduce-scatter.2.cloned.1.call-start = ((), (), s32[]{:S(2)}) async-start(), calls=%async_computation.4 | async-start | bytes 7077888 | tf_op jit(solution)/shard_map/reduce_scatter | solution.py:294
  180.5 2.7 %collective-permute-start.3 = (bf16[2,3,256,256]{3,2,1,0:T(8,128)(2,1)}, bf16[2,3,256,256]{3,2,1,0:T(8,128)(2,1)S(1)}, u32[]{:S(2)}, u32[]{:S(2)}) collective-permute-start(bf16[2,3,256,256]{3,2,1,0:T(8,128)(2,1)} %bitcast.20), channel_id=1, source_target_pairs={{0,1},{1,0},{2,3},{3,2},{4,5},{5,4},{6,7},{7,6},{8,9},{9,8},{10,11... | collective-permute-start | bytes 2359304 | tf_op jit(solution)/shard_map/ppermute | solution.py:305
Sparse Core Ops, SparseCore 0:
  15.3 75.1 all-gather.1
  106.7 73.7 reduce-scatter.1

commit v4 on v3

--- a/solution.py
+++ b/solution.py
@@ -116,22 +116,22 @@
     w_copies = [[[pltpu.make_async_copy(w_in.at[d, q, m], w_ref.at[q, m, d], w_sem.at[q, m, d])
                   for d in range(8)] for m in range(3)] for q in range(2)]
     batches = (
-        x_copies + w_copies[0][0] + w_copies[0][1],
-        w_copies[1][0] + w_copies[1][1],
+        x_copies + w_copies[0][0],
+        w_copies[0][1] + w_copies[1][0] + w_copies[1][1],
         dy_copies + w_copies[0][2] + w_copies[1][2],
     )
     for batch in batches:
         for copy in batch:
             copy.start()
     picks = [rest_pick(k) for k in range(4)]
-    for q in range(2):
-        for copy in batches[q]:
-            copy.wait()
-        if q == 0:
-            spread_rest(x_ref, left_ref.at[0], picks)
-        x = x_ref[...].reshape(ROWS, D)
-        pre_ref[q, 0] = dot(x, w_ref[q, 0].reshape(D, CB))
-        pre_ref[q, 1] = dot(x, w_ref[q, 1].reshape(D, CB))
+    for copy in batches[0]:
+        copy.wait()
+    spread_rest(x_ref, left_ref.at[0], picks)
+    pre_ref[0, 0] = dot(x_ref[...].reshape(ROWS, D), w_ref[0, 0].reshape(D, CB))
+    for copy in batches[1]:
+        copy.wait()
+    for q, m in ((0, 1), (1, 0), (1, 1)):
+        pre_ref[q, m] = dot(x_ref[...].reshape(ROWS, D), w_ref[q, m].reshape(D, CB))
     for copy in batches[2]:
         copy.wait()
     spread_rest(dy_ref, left_ref.at[1], picks)
@@ -156,8 +156,8 @@
             for m in range(3):
                 grad_ref[d, q, m] = grad_block(rows_refs[m], side_ref.at[q, m], cols)
         outs.append(pltpu.make_async_copy(grad_ref.at[d], grad_out.at[d], out_sem.at[d]))
-        if d % 2 == 1:
-            for copy in outs[-2:] if d > 1 else outs:
+        if d == 1 or d == 3 or d >= 5:
+            for copy in outs if d == 1 else outs[-2:] if d < 6 else outs[-1:]:
                 copy.start()
     for copy in outs:
         copy.wait()

time: 193 us -> 194 us (level)
  no operation moved by 1% of the time
where the time goes in v4:
time: 194 us
  blocking collectives  112 us (58%)
  Pallas kernels  35.4 us (18%)
  waiting for transfers between devices  21.2 us (11%)
  between operations  14.1 us (7%)
  other arithmetic  5.77 us (3%)
  starting transfers between devices  4.53 us (2%)
    all_to_all x1, blocking collectives, per_device(): lax.all_to_all(sent.reshape(SRC, 20 * MAIN, CB), 'eslice', 0, 0, tiled=True)  67.5 us
    all_to_all x1, blocking collectives, per_device(): returned = lax.all_to_all(back, 'eslice', 0, 0, tiled=True)  44.3 us
    pallas_call x4, Pallas kernels, call(): pl.pallas_call(kernel, out_shape=tuple(outs), in_specs=[pl.BlockSpec(memo...  35.4 us
    reduce_scatter x1, waiting for transfers between devices, per_device(): reduced = lax.psum_scatter(grads, 'dp', scatter_dimension=0, tiled=False)  15.9 us
  transfers between devices with their start and end apart: 6, of which 3 were waited for; matrix products, arithmetic and copies ran while one was open for 2% of the time, Pallas kernels for 7%

profile of v4, /device:TPU:1, one launch (start us, length us, event | category | flops | bytes accessed | tf_op | source)
XLA Modules:
  0.0 193.8 jit_solution(4394690383834396209)
XLA Ops:
  7.2 0.0 all-gather.2.cloned.1.call-start
  7.2 3.3 %collective-permute-start = (bf16[2,256,256]{2,1,0:T(8,128)(2,1)}, bf16[2,256,256]{2,1,0:T(8,128)(2,1)S(1)}, u32[]{:S(2)}, u32[]{:S(2)}) collective-permute-start(bf16[2,256,256]{2,1,0:T(8,128)(2,1)} %param.11), channel_id=1, source_target_pairs={{0,1},{1,0},{2,3},{3,2},{4,5},{5,4},{6,7},{7,6},{8,9},{9,8},{10,11... | collective-permute-start | bytes 786440 | tf_op jit(solution)/shard_map/ppermute | solution.py:273
  10.5 0.1 collective-permute-start.1
  10.6 0.4 collective-permute-start.2
  11.0 1.0 select_dynamic-update-slice_fusion.2
  12.1 1.0 select_dynamic-update-slice_fusion.1
  13.1 1.0 select_dynamic-update-slice_fusion
  14.1 0.0 collective-permute-done
  14.1 0.0 collective-permute-done.1
  14.2 0.0 collective-permute-done.2
  14.2 0.0 copy-start
  14.2 0.9 copy-done
  15.1 0.0 all-gather.2.cloned.1.call-update
  15.1 0.0 reduce-scatter.2.cloned.1.call-start
  15.2 4.7 %send.1 = bf16[8,2,2,320,256]{4,3,2,1,0:T(8,128)(2,1)} custom-call(s32[2,128]{1,0:T(2,128)} %bitcast.22, bf16[2,128]{1,0:T(2,128)(2,1)} %bitcast.24, bf16[128,2048]{1,0:T(8,128)(2,1)} %x_ref.1, bf16[128,2048]{1,0:T(8,128)(2,1)} %dy_ref.1), custom_call_target="tpu_custom_call" | custom-call | flops 1000000000 | bytes 6291456 | tf_op jit(solution)/shard_map/send/pallas_call | solution.py:253
  19.8 67.5 %all_to_all.10.rows_in = bf16[32,320,256]{2,1,0:T(8,128)(2,1)} all-to-all(bf16[32,320,256]{2,1,0:T(8,128)(2,1)} %bitcast.18), channel_id=1, replica_groups=mesh['dp'=8,'eslice'=32] {'eslice'}, dimensions={0} | all-to-all | bytes 10485760 | tf_op jit(solution)/shard_map/all_to_all | solution.py:281
  87.3 3.2 %all-gather.2.cloned.1.call-done.w_in = bf16[8,2,3,256,256]{4,3,2,1,0:T(8,128)(2,1)} async-done(((bf16[1,2,3,256,256]{4,3,2,1,0:T(8,128)(2,1)}), bf16[8,2,3,256,256]{4,3,2,1,0:T(8,128)(2,1)}) %all-gather.2.cloned.1.call-update) | async-done | bytes 6291472 | tf_op jit(solution)/shard_map/all_gather | solution.py:276
  90.5 17.1 %main.1 = (bf16[2,2,640,256]{3,2,1,0:T(8,128)(2,1)}, f32[640,128]{1,0:T(8,128)}, bf16[8,2,3,256,256]{4,3,2,1,0:T(8,128)(2,1)}) custom-call(bf16[32,320,256]{2,1,0:T(8,128)(2,1)} %all_to_all.10.rows_in, bf16[8,2,3,256,256]{4,3,2,1,0:T(8,128)(2,1)} %all-gather.2.cloned.1.call-done.w_in), custom_call_target="tpu_custom_call" | custom-call | flops 8000000000 | bytes 25165824 | tf_op jit(solution)/shard_map/main/pallas_call | solution.py:253
  107.6 0.0 reduce-scatter.2.cloned.1.call-update
  107.7 9.8 %back.1 = bf16[32,176,256]{2,1,0:T(8,128)(2,1)} custom-call(bf16[8,2,3,256,256]{4,3,2,1,0:T(8,128)(2,1)} %all-gather.2.cloned.1.call-done.w_in, bf16[2,2,640,256]{3,2,1,0:T(8,128)(2,1)} %get-tuple-element.13.side_in, f32[640,128]{1,0:T(8,128)} %get-tuple-element.14.gate_in), custom_call_target="tpu_custom_call" | custom-call | flops 3000000000 | bytes 10485760 | tf_op jit(solution)/shard_map/back/pallas_call | solution.py:253
  117.4 44.3 %all_to_all.11.back_ref = bf16[32,176,256]{2,1,0:T(8,128)(2,1)} all-to-all(bf16[32,176,256]{2,1,0:T(8,128)(2,1)} %back.1), channel_id=1, replica_groups=mesh['dp'=8,'eslice'=32] {'eslice'}, dimensions={0} | all-to-all | bytes 5767168 | tf_op jit(solution)/shard_map/all_to_all | solution.py:301
  161.8 3.9 %combine.1 = (bf16[128,2048]{1,0:T(8,128)(2,1)}, f32[2,128]{1,0:T(2,128)}) custom-call(s32[2,128]{1,0:T(2,128)} %bitcast.23, bf16[2,128]{1,0:T(2,128)(2,1)} %bitcast.25, bf16[32,176,256]{2,1,0:T(8,128)(2,1)} %all_to_all.11.back_ref), custom_call_target="tpu_custom_call" | custom-call | flops 1000000000 | bytes 4194304 | tf_op jit(solution)/shard_map/combine/pallas_call | solution.py:253
  165.7 15.9 %reduce-scatter.2.cloned.1.call-done = bf16[1,2,3,256,256]{4,3,2,1,0:T(8,128)(2,1)} async-done(((bf16[8,2,3,256,256]{4,3,2,1,0:T(8,128)(2,1)}), bf16[1,2,3,256,256]{4,3,2,1,0:T(8,128)(2,1)}) %reduce-scatter.2.cloned.1.call-update) | async-done | bytes 786448 | tf_op jit(solution)/shard_map/reduce_scatter | solution.py:294
  181.6 0.6 collective-permute-start.3
  182.2 2.1 %collective-permute-done.3 = bf16[2,3,256,256]{3,2,1,0:T(8,128)(2,1)S(1)} collective-permute-done((bf16[2,3,256,256]{3,2,1,0:T(8,128)(2,1)}, bf16[2,3,256,256]{3,2,1,0:T(8,128)(2,1)S(1)}, u32[]{:S(2)}, u32[]{:S(2)}) %collective-permute-start.3) | collective-permute-done | bytes 786464 | tf_op jit(solution)/shard_map/ppermute | solution.py:305
  184.3 1.1 select_bitcast_fusion.1
  185.4 0.7 pad_maximum_fusion.2
  186.1 0.8 pad_maximum_fusion
  (3 shorter events, 0.1 us)
Async XLA Ops:
  7.2 83.3 %all-gather.2.cloned.1.call-start = ((), (), s32[]{:S(2)}) async-start(), calls=%async_computation.3 | async-start | bytes 7077888 | tf_op jit(solution)/shard_map/all_gather | solution.py:276
  7.2 6.9 %collective-permute-start = (bf16[2,256,256]{2,1,0:T(8,128)(2,1)}, bf16[2,256,256]{2,1,0:T(8,128)(2,1)S(1)}, u32[]{:S(2)}, u32[]{:S(2)}) collective-permute-start(bf16[2,256,256]{2,1,0:T(8,128)(2,1)} %param.11), channel_id=1, source_target_pairs={{0,1},{1,0},{2,3},{3,2},{4,5},{5,4},{6,7},{7,6},{8,9},{9,8},{10,11... | collective-permute-start | bytes 786440 | tf_op jit(solution)/shard_map/ppermute | solution.py:273
  10.5 3.6 %collective-permute-start.1 = (bf16[2,256,256]{2,1,0:T(8,128)(2,1)}, bf16[2,256,256]{2,1,0:T(8,128)(2,1)S(1)}, u32[]{:S(2)}, u32[]{:S(2)}) collective-permute-start(bf16[2,256,256]{2,1,0:T(8,128)(2,1)} %param.12), channel_id=1, source_target_pairs={{0,1},{1,0},{2,3},{3,2},{4,5},{5,4},{6,7},{7,6},{8,9},{9,8},{10,11... | collective-permute-start | bytes 786440 | tf_op jit(solution)/shard_map/ppermute | solution.py:273
  10.6 3.5 %collective-permute-start.2 = (bf16[2,256,256]{2,1,0:T(8,128)(2,1)}, bf16[2,256,256]{2,1,0:T(8,128)(2,1)S(1)}, u32[]{:S(2)}, u32[]{:S(2)}) collective-permute-start(bf16[2,256,256]{2,1,0:T(8,128)(2,1)} %param.13), channel_id=1, source_target_pairs={{0,1},{1,0},{2,3},{3,2},{4,5},{5,4},{6,7},{7,6},{8,9},{9,8},{10,11... | collective-permute-start | bytes 786440 | tf_op jit(solution)/shard_map/ppermute | solution.py:273
  14.2 0.9 copy-start
  15.1 166.4 %reduce-scatter.2.cloned.1.call-start = ((), (), s32[]{:S(2)}) async-start(), calls=%async_computation.4 | async-start | bytes 7077888 | tf_op jit(solution)/shard_map/reduce_scatter | solution.py:294
  181.6 2.7 %collective-permute-start.3 = (bf16[2,3,256,256]{3,2,1,0:T(8,128)(2,1)}, bf16[2,3,256,256]{3,2,1,0:T(8,128)(2,1)S(1)}, u32[]{:S(2)}, u32[]{:S(2)}) collective-permute-start(bf16[2,3,256,256]{3,2,1,0:T(8,128)(2,1)} %bitcast.20), channel_id=1, source_target_pairs={{0,1},{1,0},{2,3},{3,2},{4,5},{5,4},{6,7},{7,6},{8,9},{9,8},{10,11... | collective-permute-start | bytes 2359304 | tf_op jit(solution)/shard_map/ppermute | solution.py:305
Sparse Core Ops, SparseCore 0:
  15.3 75.1 all-gather.1
  107.8 73.7 reduce-scatter.1
